TPU v7x, 32 devices: a whole 2x2x4 slice. The times are simulated.
32 devices in a mesh: dp: 4 (over y, x), mp: 8 (over z, core).
Axes of the slice: x: 2, y: 2, z: 4, core: 2. Of those that a mesh axis runs over, the one named last changes fastest.
Arguments:
- hidden: bfloat16 [32, 128, 18432], P('dp', None, 'mp'), may hold values from -400 to 400
- cotangent: bfloat16 [32, 128, 4608], P('dp', 'mp'), may hold values from -8 to 8
- w_down: bfloat16 [18432, 4608], P('mp', 'dp'), may hold values from -0.046875 to 0.046875
- lengths: int32 [32], P('dp'), may hold values from 1 to 128, 3072 in all
Outputs:
- weight_grad: float32 [18432, 4608], P('mp', 'dp')
- d_hidden: bfloat16 [32, 128, 18432], P('dp', None, 'mp')
All inputs are finite; a program needn't handle non-finite values. No bound on the sum of `lengths` on one device may be relied on, other than what follows from the above.
Results may differ from a plain program's by a relative error of at most 0.003.
Values may be sent and summed in bfloat16 or wider, within the bound.
A program may use at most 448 MiB of HBM per device.

v0:
```python
import math

import jax
import jax.numpy as jnp
from jax import lax
from jax.sharding import PartitionSpec as P


def body(hidden, cotangent, w_down, lengths):
    seqs = hidden.shape[0]
    whole = lax.all_gather(cotangent, "mp", axis=1, tiled=True)
    seq_len = whole.shape[1]
    width = whole.shape[2]
    positions = jnp.arange(seq_len, dtype=jnp.int32)
    keep = positions[None, :] < lengths[:, None]
    masked = jnp.where(keep[:, :, None], whole, jnp.zeros((), whole.dtype))
    flat = masked.reshape(seqs * seq_len, width)
    units = hidden.shape[2]
    part = flat
    grads_in = lax.dot_general(
        part,
        lax.all_gather(w_down, "dp", axis=1, tiled=True),
        (((1,), (1,)), ((), ())),
        preferred_element_type=jnp.float32,
    )
    d_hidden = grads_in.astype(jnp.bfloat16).reshape(seqs, seq_len, units)
    cot_gram = jnp.einsum("bsd,btd->bst", masked, masked, preferred_element_type=jnp.float32)
    hid_gram = jnp.einsum("bsf,btf->bst", hidden, hidden, preferred_element_type=jnp.float32)
    sq_norm = lax.psum(jnp.sum(hid_gram * cot_gram, axis=(1, 2)), "mp")
    full_units = units * lax.axis_size("mp")
    groups = lax.axis_size("dp")
    radius = math.sqrt(full_units * width / (seqs * groups))
    clip_scale = radius / jnp.sqrt(sq_norm + 1e-06)
    share = width // groups
    running = jnp.zeros((share * lax.axis_size("dp"), units), jnp.float32)
    for which in range(seqs):
        part = masked[which]
        running = running + clip_scale[which] * lax.dot_general(
            part, hidden[which], (((0,), (0,)), ((), ())), preferred_element_type=jnp.float32
        )
    local = lax.psum_scatter(running, "dp", scatter_dimension=0, tiled=True)
    weight_grad = local.T
    return (weight_grad, d_hidden)


def solution(mesh):
    in_specs = (P("dp", None, "mp"), P("dp", "mp", None), P("mp", "dp"), P("dp"))
    out_specs = (P("mp", "dp"), P("dp", None, "mp"))
    return jax.shard_map(body, mesh=mesh, in_specs=in_specs, out_specs=out_specs, check_vma=False)
```

profile of v0, /device:TPU:0, one launch (start us, length us, event | category | flops | bytes accessed | tf_op | source)
XLA Modules:
  0.0 753.4 jit_solution(11671920220366567995)
XLA Ops:
  7.2 0.0 all-gather.3.cloned.1.call-start
  7.2 0.7 all-gather.3.cloned.1.call-update
  7.9 0.0 all-gather.5.cloned.1.call-start
  7.9 0.7 all-gather.5.cloned.1.call-update
  8.6 0.0 reduce-scatter.2.cloned.1.call-start
  8.7 0.7 iota_compare_fusion
  9.4 5.2 fusion.25
  14.6 88.5 %all-gather.3.cloned.1.call-done = bf16[8,128,4608]{2,1,0:T(8,128)(2,1)} async-done(((bf16[8,16,4608]{2,1,0:T(8,128)(2,1)}), bf16[8,128,4608]{2,1,0:T(8,128)(2,1)}) %all-gather.3.cloned.1.call-update) | async-done | bytes 9437200 | tf_op jit(solution)/shard_map/all_gather | solution.py:11
  103.1 9.2 %broadcast_select_fusion = bf16[8,128,4608]{2,1,0:T(8,128)(2,1)} fusion(bf16[8,128,4608]{2,1,0:T(8,128)(2,1)} %all-gather.3.cloned.1.call-done, pred[8,128]{1,0:T(8,128)(4,1)S(1)} %iota_compare_fusion), kind=kLoop, calls=%fused_computation.1 | loop fusion | flops 4718592 | bytes 18875392 | tf_op jit(solution)/shard_map/jit(_where)/select_n | solution.py:16
  112.3 0.0 slice-start
  112.3 12.7 %fusion.7 = f32[8]{0:T(128)S(1)} fusion(f32[8,128,128]{2,1,0:T(8,128)S(1)} %fusion.25, bf16[8,128,4608]{2,1,0:T(8,128)(2,1)} %broadcast_select_fusion), kind=kOutput, calls=%fused_computation.19 | convolution fusion | flops 1208221696 | bytes 9961504 | tf_op jit(solution)/shard_map/bsd,btd->bst/dot_general | solution.py:27
  125.0 14.0 %psum.7 = f32[8]{0:T(128)S(1)} all-reduce(f32[8]{0:T(128)S(1)} %fusion.7), channel_id=1, replica_groups=mesh['dp'=4,'mp'=8] {'mp'}, use_global_device_ids=true, to_apply=%region_1.2 | all-reduce | flops 8 | bytes 64 | tf_op jit(solution)/shard_map/psum | solution.py:29
  139.0 0.7 fusion.24
  139.7 0.0 slice-start.1
  139.7 0.0 slice-start.2
  139.7 17.9 %fusion = f32[4608,2304]{1,0:T(8,128)} fusion(bf16[8,128,4608]{2,1,0:T(8,128)(2,1)} %broadcast_select_fusion, bf16[8,128,2304]{2,1,0:T(8,128)(2,1)} %param.4), kind=kOutput, calls=%fused_computation.6 | convolution fusion | flops 2717908992 | bytes 44236800 | tf_op jit(solution)/shard_map/dot_general | solution.py:38
  157.5 0.0 slice-done
  157.5 0.0 slice-done.1
  157.5 0.0 slice-done.2
  157.6 17.5 %fusion.1 = f32[4608,2304]{1,0:T(8,128)} fusion(bf16[8,128,4608]{2,1,0:T(8,128)(2,1)S(1)} %bitcast.73, bf16[8,128,2304]{2,1,0:T(8,128)(2,1)} %param.4), kind=kOutput, calls=%fused_computation.8 | convolution fusion | flops 2717908992 | bytes 44236800 | tf_op jit(solution)/shard_map/dot_general | solution.py:38
  175.0 21.0 %fusion.2 = f32[4608,2304]{1,0:T(8,128)} fusion(bf16[8,128,4608]{2,1,0:T(8,128)(2,1)S(1)} %bitcast.73, bf16[8,128,2304]{2,1,0:T(8,128)(2,1)} %param.4), kind=kOutput, calls=%fused_computation.10 | convolution fusion | flops 2717908992 | bytes 44236800 | tf_op jit(solution)/shard_map/dot_general | solution.py:38
  196.0 17.5 %fusion.3 = f32[4608,2304]{1,0:T(8,128)} fusion(bf16[8,128,4608]{2,1,0:T(8,128)(2,1)S(1)} %bitcast.73, bf16[8,128,2304]{2,1,0:T(8,128)(2,1)} %param.4), kind=kOutput, calls=%fused_computation.12 | convolution fusion | flops 2717908992 | bytes 44236800 | tf_op jit(solution)/shard_map/dot_general | solution.py:38
  213.5 17.4 %fusion.4 = f32[4608,2304]{1,0:T(8,128)} fusion(bf16[8,128,4608]{2,1,0:T(8,128)(2,1)S(1)} %bitcast.73, bf16[8,128,2304]{2,1,0:T(8,128)(2,1)} %param.4), kind=kOutput, calls=%fused_computation.14 | convolution fusion | flops 2717908992 | bytes 44236800 | tf_op jit(solution)/shard_map/dot_general | solution.py:38
  231.0 17.5 %fusion.5 = f32[4608,2304]{1,0:T(8,128)} fusion(bf16[8,128,4608]{2,1,0:T(8,128)(2,1)S(1)} %bitcast.73, bf16[8,128,2304]{2,1,0:T(8,128)(2,1)} %param.4), kind=kOutput, calls=%fused_computation.16 | convolution fusion | flops 2717908992 | bytes 44236800 | tf_op jit(solution)/shard_map/dot_general | solution.py:38
  248.5 17.5 %fusion.6 = f32[4608,2304]{1,0:T(8,128)} fusion(bf16[8,128,4608]{2,1,0:T(8,128)(2,1)S(1)} %bitcast.73, bf16[8,128,2304]{2,1,0:T(8,128)(2,1)} %param.4), kind=kOutput, calls=%fused_computation.18 | convolution fusion | flops 2717908992 | bytes 44236800 | tf_op jit(solution)/shard_map/dot_general | solution.py:38
  266.0 109.4 %multiply_add_fusion = f32[4608,2304]{1,0:T(8,128)} fusion(f32[4608,2304]{1,0:T(8,128)} %fusion, f32[4608,2304]{1,0:T(8,128)} %fusion.1, f32[4608,2304]{1,0:T(8,128)} %fusion.2, f32[4608,2304]{1,0:T(8,128)} %fusion.3, f32[4608,2304]{1,0:T(8,128)} %fusion.4, f32[4608,2304]{1,0:T(8,128)} %fusion.5, f32[4608,2304]{1,0:T(8,128)} %fusion.6, f32[]{:T(128)} %bitcast.21, ...), kind=kOutput, calls=%fused_computation | convolution fusion | flops 2877161472 | bytes 341512192 | tf_op jit(solution)/shard_map/dot_general | solution.py:38
  375.4 0.0 reduce-scatter.2.cloned.1.call-update
  375.4 0.0 all-gather.5.cloned.1.call-done
  375.5 30.2 %convolution_convert_fusion = bf16[1024,2304]{1,0:T(8,128)(2,1)} fusion(bf16[1024,4608]{1,0:T(8,128)(2,1)} %bitcast.71, bf16[2304,4608]{1,0:T(8,128)(2,1)} %all-gather.5.cloned.1.call-done), kind=kOutput, calls=%fused_computation.2 | convolution fusion | flops 21745631232 | bytes 35389440 | tf_op jit(solution)/shard_map/dot_general | solution.py:20
  405.6 328.6 %reduce-scatter.2.cloned.1.call-done = f32[1152,2304]{1,0:T(8,128)} async-done(((f32[4608,2304]{1,0:T(8,128)}), f32[1152,2304]{1,0:T(8,128)}) %reduce-scatter.2.cloned.1.call-update) | async-done | bytes 10616848 | tf_op jit(solution)/shard_map/reduce_scatter | solution.py:41
  734.3 12.7 %copy.6 = f32[2304,1152]{1,0:T(8,128)} copy(f32[2304,1152]{0,1:T(8,128)} %bitcast.74) | data formatting | bytes 21233664
  (2 shorter events, 0.0 us)
Async XLA Ops:
  7.2 95.9 %all-gather.3.cloned.1.call-start = ((), (), s32[]{:S(2)}) async-start(), calls=%async_computation.1 | async-start | bytes 10616832 | tf_op jit(solution)/shard_map/all_gather | solution.py:11
  7.9 367.5 %all-gather.5.cloned.1.call-start = ((), (), s32[]{:S(2)}) async-start(), calls=%async_computation.3 | async-start | bytes 26542080 | tf_op jit(solution)/shard_map/all_gather | solution.py:22
  8.6 725.6 %reduce-scatter.2.cloned.1.call-start = ((), (), s32[]{:S(2)}) async-start(), calls=%async_computation.2 | async-start | bytes 53084160 | tf_op jit(solution)/shard_map/reduce_scatter | solution.py:41
  112.3 45.3 %slice-start = ((s8[9437184]{0:T(1024)(128)(4,1)}), s8[1048576]{0:T(1024)(128)(4,1)S(1)}, s32[]{:S(2)}) async-start(s8[9437184]{0:T(1024)(128)(4,1)} %bitcast.72), calls=%async_computation.4 | async-start | bytes 2097152
  139.7 17.9 %slice-start.1 = ((s8[9437184]{0:T(1024)(128)(4,1)}), s8[4194304]{0:T(1024)(128)(4,1)S(1)}, s32[]{:S(2)}) async-start(s8[9437184]{0:T(1024)(128)(4,1)} %bitcast.72), calls=%async_computation.5 | async-start | bytes 8388608
  139.7 17.9 %slice-start.2 = ((s8[9437184]{0:T(1024)(128)(4,1)}), s8[4194304]{0:T(1024)(128)(4,1)S(1)}, s32[]{:S(2)}) async-start(s8[9437184]{0:T(1024)(128)(4,1)} %bitcast.72), calls=%async_computation.6 | async-start | bytes 8388608
Sparse Core Ops, SparseCore 0:
  9.6 93.4 all-gather.2
  104.9 193.7 all-gather.4
  375.5 358.6 reduce-scatter.1
where the time goes:
time: 754 us; the launch traced here: 753 us
  waiting for transfers between devices  419 us (56%)
  matrix products  284 us (38%)
  blocking collectives  14 us (2%)
  between operations  13.8 us (2%)
  local copies, waits for them, and re-layouts  13.3 us (2%)
  other arithmetic  9.95 us (1%)
    reduce_scatter x1, waiting for transfers between devices, body(): local = lax.psum_scatter(running, 'dp', scatter_dimension=0, tiled=True)  329 us
    dot_general x8, matrix products, body(): lax.dot_general(part, hidden[which], (((0,), (0,)), ((), ())), preferred_...  236 us
    all_gather x1, waiting for transfers between devices, body(): whole = lax.all_gather(cotangent, 'mp', axis=1, tiled=True)  88.5 us
    dot_general x1, matrix products, body(): lax.dot_general(part, lax.all_gather(w_down, 'dp', axis=1, tiled=True), (...  30.2 us
  transfers between devices with their start and end apart: 3, of which 2 were waited for; matrix products, arithmetic and copies ran while one was open for 39% of the time, Pallas kernels for 0%

commit v1 on v0

v1 whole, which is shorter than its diff:
```python
import math

import jax
import jax.numpy as jnp
from jax import lax
from jax.sharding import PartitionSpec as P

F32 = jnp.float32
BF16 = jnp.bfloat16


def total_over(value, axis):
    size = lax.axis_size(axis)
    if size & (size - 1):
        return lax.psum(value, axis)
    step = 1
    while step < size:
        value = value + lax.ppermute(value, axis, [(i, i ^ step) for i in range(size)])
        step *= 2
    return value


def pieces(extent, count):
    while extent % (count * 128):
        count -= 1
        if count == 1:
            break
    size = extent // count
    return [(i * size, (i + 1) * size) for i in range(count)]


def body(hidden, cotangent, w_down, lengths):
    seqs, chunk, width = cotangent.shape
    units = hidden.shape[2]
    groups = lax.axis_size("dp")
    ranks = lax.axis_size("mp")
    seq_len = chunk * ranks
    share = width // groups
    inner = 2 if groups % 2 == 0 else 1
    outer = groups // inner
    me = lax.axis_index("dp")
    row, col = me // inner, me % inner

    def along_inner(value, k):
        perm = [(r * inner + c, r * inner + (c + k) % inner) for r in range(outer) for c in range(inner)]
        return lax.ppermute(value, "dp", perm)

    def along_outer(value, m):
        perm = [(r * inner + c, (r + m) % outer * inner + c) for r in range(outer) for c in range(inner)]
        return lax.ppermute(value, "dp", perm)

    def columns_of(c):
        blocks = [
            lax.dynamic_slice_in_dim(cotangent, ((row - m) % outer * inner + c) * share, share, 2)
            for m in range(outer)
        ]
        return jnp.concatenate(blocks, axis=2)

    cot_parts = [columns_of(col)]
    for k in range(1, inner):
        cot_parts.append(along_inner(columns_of((col + k) % inner), k))
    held, *cot_parts = lax.optimization_barrier((hidden, *cot_parts))

    w_parts = [w_down] + [along_outer(w_down, m) for m in range(1, outer)]
    hid_parts = [hidden] + [along_inner(held, k) for k in range(1, inner)]
    len_parts = [lengths] + [along_inner(lengths, k) for k in range(1, inner)]

    positions = jnp.arange(seq_len, dtype=jnp.int32)

    def masked_by(value, keep):
        return jnp.where(keep[:, :, None], value, jnp.zeros((), value.dtype))

    keeps = [positions[None, :] < n[:, None] for n in len_parts]

    slim = lax.all_to_all(cotangent, "mp", split_axis=2, concat_axis=1, tiled=True)
    slim = masked_by(slim, keeps[0])
    cot_gram = total_over(jnp.einsum("bsd,btd->bst", slim, slim, preferred_element_type=F32), "mp")
    hid_gram = jnp.einsum("bsf,btf->bst", hidden, hidden, preferred_element_type=F32)
    sq_norm = total_over(jnp.sum(hid_gram * cot_gram, axis=(1, 2)), "mp")
    radius = math.sqrt(units * ranks * width / (seqs * groups))
    clip = radius / jnp.sqrt(sq_norm + 1e-06)
    clips = [clip] + [along_inner(clip, k) for k in range(1, inner)]

    whole = lax.all_gather(jnp.stack(cot_parts), "mp", axis=2, tiled=True)
    masked = [masked_by(whole[k], keeps[k]) for k in range(inner)]
    tokens = seqs * seq_len

    def grad_w(m, lo, hi):
        total = None
        for k in range(inner):
            part = masked[k][:, :, m * share:(m + 1) * share]
            scaled = (part.astype(F32) * clips[k][:, None, None]).astype(BF16)
            term = lax.dot_general(
                hid_parts[k][:, :, lo:hi].reshape(tokens, hi - lo),
                scaled.reshape(tokens, share),
                (((0,), (0,)), ((), ())),
                preferred_element_type=F32,
            )
            total = term if total is None else total + term
        return total

    def grad_h(k, lo, hi):
        total = None
        for m in range(outer):
            term = lax.dot_general(
                masked[k][:, :, m * share:(m + 1) * share].reshape(tokens, share),
                w_parts[m][lo:hi],
                (((1,), (1,)), ((), ())),
                preferred_element_type=F32,
            )
            total = term if total is None else total + term
        return total

    cuts = pieces(units, 3)
    grad_w_in = [[along_outer(grad_w(m, *cut).astype(BF16), -m) for m in range(1, outer)] for cut in cuts]
    grad_h_in = [[along_inner(grad_h(k, *cut).astype(BF16), -k) for k in range(1, inner)] for cut in cuts]

    own_w, own_h = grad_w(0, 0, units), grad_h(0, 0, units)
    for k in range(inner - 1):
        own_h = own_h + jnp.concatenate([parts[k] for parts in grad_h_in], axis=1).astype(F32)
    for m in range(outer - 1):
        own_w = own_w + jnp.concatenate([parts[m] for parts in grad_w_in], axis=0).astype(F32)
    return (own_w, own_h.astype(BF16).reshape(seqs, seq_len, units))


def solution(mesh):
    in_specs = (P("dp", None, "mp"), P("dp", "mp", None), P("mp", "dp"), P("dp"))
    out_specs = (P("mp", "dp"), P("dp", None, "mp"))
    return jax.shard_map(body, mesh=mesh, in_specs=in_specs, out_specs=out_specs, check_vma=False)
```

time: 754 us -> 433 us (0.57)
  waiting for transfers between devices: 419 us -> 221 us
  matrix products: 284 us -> 101 us
  local copies, waits for them, and re-layouts: 13.3 us -> 62.2 us
  starting transfers between devices: 0.11 us -> 20.9 us
  blocking collectives: 14 us -> 0 us
    reduce_scatter x1 -> x0, waiting for transfers between devices: 329 us -> none  [body(): local = lax.psum_scatter(running, 'dp', scatter_dimension=0, tiled=True)]
    dot_general x11 -> x18, matrix products: 284 us -> 101 us  [the longest x8 53.1 us: grad_w(): lax.dot_general(hid_parts[k][:, :, lo:hi].reshape(tokens, hi - lo), scale...]
    ppermute x0 -> x17, waiting for transfers between devices: none -> 164 us  [the longest x7 113 us: along_inner(): return lax.ppermute(value, 'dp', perm)]
    all_gather x2 -> x1, waiting for transfers between devices: 88.5 us -> 0.01 us  [body(): whole = lax.all_gather(jnp.stack(cot_parts), 'mp', axis=2, tiled=True)]
    all_to_all x0 -> x1, waiting for transfers between devices: none -> 57.5 us  [body(): lax.all_to_all(cotangent, 'mp', split_axis=2, concat_axis=1, tiled=True)]
    unnamed x7 -> x24, local copies, waits for them, and re-layouts: 12.7 us -> 44 us
    ppermute x0 -> x17, starting transfers between devices: none -> 15.8 us  [the longest x7 10.2 us: along_inner(): return lax.ppermute(value, 'dp', perm)]
    psum x1 -> x0, blocking collectives: 14 us -> none  [body(): sq_norm = lax.psum(jnp.sum(hid_gram * cot_gram, axis=(1, 2)), 'mp')]
  transfers between devices with their start and end apart: 3 -> 19, of which waited for: 2 -> 13; matrix products, arithmetic and copies ran while one was open for 39% -> 32% of each run, Pallas kernels for 0% -> 0%
where the time goes in v1:
time: 433 us; the launch traced here: 426 us
  waiting for transfers between devices  221 us (51%)
  matrix products  101 us (23%)
  local copies, waits for them, and re-layouts  62.2 us (14%)
  starting transfers between devices  20.9 us (5%)
  between operations  14.7 us (3%)
  other arithmetic  6.31 us (1%)
    ppermute x7, waiting for transfers between devices, along_inner(): return lax.ppermute(value, 'dp', perm)  113 us
    all_to_all x1, waiting for transfers between devices, body(): lax.all_to_all(cotangent, 'mp', split_axis=2, concat_axis=1, tiled=True)  57.5 us
    dot_general x8, matrix products, grad_w(): lax.dot_general(hid_parts[k][:, :, lo:hi].reshape(tokens, hi - lo), scale...  53.1 us
    unnamed x24, local copies, waits for them, and re-layouts  44 us
    ppermute x6, waiting for transfers between devices, total_over(): lax.ppermute(value, axis, [(i, i ^ step) for i in range(size)])  43.4 us
    dot_general x8, matrix products, grad_h(): lax.dot_general(masked[k][:, :, m * share:(m + 1) * share].reshape(tokens...  41.9 us
    ppermute x7, starting transfers between devices, along_inner(): return lax.ppermute(value, 'dp', perm)  10.2 us
    all_to_all x1, local copies, waits for them, and re-layouts, body(): lax.all_to_all(cotangent, 'mp', split_axis=2, concat_axis=1, tiled=True)  8.75 us
  transfers between devices with their start and end apart: 19, of which 13 were waited for; matrix products, arithmetic and copies ran while one was open for 32% of the time, Pallas kernels for 0%

profile of v1, /device:TPU:0, one launch (start us, length us, event | category | flops | bytes accessed | tf_op | source)
XLA Modules:
  0.0 426.2 jit_solution(15136902577742940834)
XLA Ops:
  7.3 1.3 constant_dynamic-slice_fusion.1
  8.7 3.0 collective-permute-start
  11.7 13.3 %collective-permute-done = bf16[8,16,2304]{2,1,0:T(8,128)(2,1)S(1)} collective-permute-done((bf16[8,16,2304]{2,1,0:T(8,128)(2,1)S(1)}, bf16[8,16,2304]{2,1,0:T(8,128)(2,1)S(1)}, u32[]{:S(2)}, u32[]{:S(2)}) %collective-permute-start) | collective-permute-done | bytes 589856 | tf_op jit(solution)/shard_map/ppermute | solution.py:46
  26.2 7.9 %copy.30 = bf16[8,16,4608]{1,0,2:T(8,128)(2,1)} copy(bf16[8,16,4608]{2,1,0:T(8,128)(2,1)S(1)} %copy-done.1) | data formatting | bytes 2359296 | tf_op args[1]
  34.1 12.5 %reshape.96 = bf16[8,2,36864]{2,1,0:T(2,128)(2,1)} reshape(bf16[4608,8,16]{2,1,0:T(8,128)(2,1)} %bitcast.81) | data formatting | bytes 2359296
  46.6 5.1 %all-to-all-start = ((bf16[8,2,36864]{2,1,0:T(2,128)(2,1)}), bf16[8,2,36864]{2,1,0:T(2,128)(2,1)S(1)}, u32[]{:S(2)}, u32[]{:S(2)}) async-start(bf16[8,2,36864]{2,1,0:T(2,128)(2,1)} %reshape.96), calls=%async_computation | async-start | bytes 2359296 | tf_op jit(solution)/shard_map/all_to_all | solution.py:75
  51.7 1.5 collective-permute-start.13
  53.3 57.5 %all-to-all-done = bf16[8,2,36864]{2,1,0:T(2,128)(2,1)S(1)} async-done(((bf16[8,2,36864]{2,1,0:T(2,128)(2,1)}), bf16[8,2,36864]{2,1,0:T(2,128)(2,1)S(1)}, u32[]{:S(2)}, u32[]{:S(2)}) %all-to-all-start) | async-done | bytes 1179680 | tf_op jit(solution)/shard_map/all_to_all | solution.py:75
  110.8 8.0 %reshape.97 = bf16[4608,8,16]{2,1,0:T(8,128)(2,1)} reshape(bf16[8,2,36864]{2,1,0:T(2,128)(2,1)S(1)} %all-to-all-done) | data formatting | bytes 2359296
  118.8 8.8 %copy.31 = bf16[8,16,8,576]{3,1,2,0:T(8,128)(2,1)S(1)} copy(bf16[8,16,8,576]{1,0,3,2:T(8,128)(2,1)} %bitcast.80) | data formatting | bytes 2359296 | tf_op jit(solution)/shard_map/all_to_all | solution.py:75
  128.6 1.8 collective-permute-done.1
  130.6 1.5 collective-permute-start.8
  132.1 21.1 %collective-permute-done.2 = f32[8,128,128]{2,1,0:T(8,128)S(1)} collective-permute-done((f32[8,128,128]{2,1,0:T(8,128)S(1)}, f32[8,128,128]{2,1,0:T(8,128)S(1)}, u32[]{:S(2)}, u32[]{:S(2)}) %collective-permute-start.2) | collective-permute-done | bytes 524320 | tf_op jit(solution)/shard_map/ppermute | solution.py:18
  153.3 5.1 %fusion.40 = f32[8,128,128]{2,1,0:T(8,128)S(1)} fusion(bf16[8,128,2304]{2,1,0:T(8,128)(2,1)} %param.4), kind=kOutput, calls=%fused_computation.64 | convolution fusion | flops 603979776 | bytes 5242880 | tf_op jit(solution)/shard_map/bsf,btf->bst/dot_general | solution.py:78
  158.6 6.6 %copy.35 = bf16[8,128,2304]{1,2,0:T(8,128)(2,1)} copy(bf16[8,128,2304]{2,1,0:T(8,128)(2,1)} %param.4) | data formatting | bytes 9437184 | tf_op jit(solution)/shard_map/optimization_barrier | solution.py:62
  165.2 1.5 collective-permute-start.7
  166.6 11.6 %collective-permute-done.3 = f32[8,128,128]{2,1,0:T(8,128)S(1)} collective-permute-done((f32[8,128,128]{2,1,0:T(8,128)S(1)}, f32[8,128,128]{2,1,0:T(8,128)S(1)}, u32[]{:S(2)}, u32[]{:S(2)}) %collective-permute-start.3) | collective-permute-done | bytes 524320 | tf_op jit(solution)/shard_map/ppermute | solution.py:18
  179.6 3.5 collective-permute-done.5
  183.3 4.3 %collective-permute-done.6 = f32[8]{0:T(128)S(1)} collective-permute-done((f32[8]{0:T(128)S(1)}, f32[8]{0:T(128)S(1)}, u32[]{:S(2)}, u32[]{:S(2)}) %collective-permute-start.6) | collective-permute-done | bytes 64 | tf_op jit(solution)/shard_map/ppermute | solution.py:18
  187.6 1.5 collective-permute-start.9
  189.1 4.3 %fusion.2 = (bf16[8,128,2304]{2,1,0:T(8,128)(2,1)S(1)}, bf16[8,128,2304]{2,1,0:T(8,128)(2,1)S(1)}) fusion(bf16[2,8,128,2304]{3,2,1,0:T(8,128)(2,1)} %all-gather.2.cloned.1.call-done, pred[8,128]{1,0:T(8,128)(4,1)S(1)} %iota_compare_fusion, pred[8,128]{1,0:T(8,128)(4,1)S(1)} %iota_compare_fusion.1), kind=kLoop, calls=%fused_computation.6 | loop fusion | flops 4718592 | bytes 18876416 | tf_op jit(solution)/shard_map/jit(_where)/select_n | solution.py:71
  193.5 1.5 fusion.38
  195.7 2.2 fusion.22
  197.9 4.9 %add_convert_fusion.3 = bf16[1024,768]{1,0:T(8,128)(2,1)} fusion(f32[1024,768]{1,0:T(8,128)S(1)} %fusion.22, bf16[1024,1152]{1,0:T(8,128)(2,1)S(1)} %bitcast.84, bf16[2304,1152]{1,0:T(8,128)(2,1)} %collective-permute-done.13), kind=kOutput, calls=%fused_computation.27 | convolution fusion | flops 1813512192 | bytes 8847360 | tf_op jit(solution)/shard_map/dot_general | solution.py:105
  202.8 2.2 fusion.20
  205.7 4.9 %add_convert_fusion.2 = bf16[1024,768]{1,0:T(8,128)(2,1)} fusion(f32[1024,768]{1,0:T(8,128)S(1)} %fusion.20, bf16[1024,1152]{1,0:T(8,128)(2,1)S(1)} %bitcast.85, bf16[2304,1152]{1,0:T(8,128)(2,1)} %collective-permute-done.13), kind=kOutput, calls=%fused_computation.26 | convolution fusion | flops 1813512192 | bytes 8847360 | tf_op jit(solution)/shard_map/dot_general | solution.py:105
  210.5 1.5 collective-permute-start.15
  212.0 2.2 fusion.18
  214.3 3.8 add_convert_fusion.1
  218.7 4.0 convolution_bitcast_fusion.7
  222.7 3.9 convolution_bitcast_fusion.5
  226.6 8.5 %convolution_bitcast_fusion.1 = f32[2304,1152]{0,1:T(8,128)} fusion(bf16[8,128,2304]{2,1,0:T(8,128)(2,1)S(1)} %bitcast.79, f32[8]{0:T(128)S(1)} %rsqrt_multiply_fusion, bf16[8,128,2304]{2,1,0:T(8,128)(2,1)S(1)} %get-tuple-element.15), kind=kOutput, calls=%fused_computation.3 | convolution fusion | flops 5439356928 | bytes 17695232 | tf_op jit(solution)/shard_map/dot_general | solution.py:93
  235.1 35.1 %collective-permute-done.9 = f32[8]{0:T(128)S(1)} collective-permute-done((f32[8]{0:T(128)S(1)}, f32[8]{0:T(128)S(1)}, u32[]{:S(2)}, u32[]{:S(2)}) %collective-permute-start.9) | collective-permute-done | bytes 64 | tf_op jit(solution)/shard_map/ppermute | solution.py:46
  270.2 5.9 %fusion.7 = bf16[768,1152]{0,1:T(8,128)(2,1)} fusion(f32[768,1152]{0,1:T(8,128)} %convolution_bitcast_fusion.7, bf16[8,128,2304]{1,2,0:T(8,128)(2,1)} %collective-permute-done.7, f32[8]{0:T(128)S(1)} %collective-permute-done.9, bf16[8,128,2304]{2,1,0:T(8,128)(2,1)S(1)} %get-tuple-element.14), kind=kOutput, calls=%fused_computation.22 | convolution fusion | flops 1817247744 | bytes 9241088 | tf_op jit(solution)/shard_map/dot_general | solution.py:93
  276.1 1.5 collective-permute-start.10
  277.5 5.9 %fusion.8 = bf16[768,1152]{0,1:T(8,128)(2,1)} fusion(f32[768,1152]{0,1:T(8,128)} %convolution_bitcast_fusion.5, bf16[8,128,2304]{1,2,0:T(8,128)(2,1)} %collective-permute-done.7, f32[8]{0:T(128)S(1)} %collective-permute-done.9, bf16[8,128,2304]{2,1,0:T(8,128)(2,1)S(1)} %get-tuple-element.14), kind=kOutput, calls=%fused_computation.23 | convolution fusion | flops 1817247744 | bytes 9241088 | tf_op jit(solution)/shard_map/dot_general | solution.py:93
  284.0 4.0 convolution_bitcast_fusion.3
  288.0 5.9 %fusion.9 = bf16[768,1152]{0,1:T(8,128)(2,1)} fusion(f32[768,1152]{0,1:T(8,128)} %convolution_bitcast_fusion.3, bf16[8,128,2304]{1,2,0:T(8,128)(2,1)} %collective-permute-done.7, f32[8]{0:T(128)S(1)} %collective-permute-done.9, bf16[8,128,2304]{2,1,0:T(8,128)(2,1)S(1)} %get-tuple-element.14), kind=kOutput, calls=%fused_computation.24 | convolution fusion | flops 1817247744 | bytes 9241088 | tf_op jit(solution)/shard_map/dot_general | solution.py:93
  293.9 9.9 %collective-permute-done.14 = bf16[1024,768]{1,0:T(8,128)(2,1)S(1)} collective-permute-done((bf16[1024,768]{1,0:T(8,128)(2,1)}, bf16[1024,768]{1,0:T(8,128)(2,1)S(1)}, u32[]{:S(2)}, u32[]{:S(2)}) %collective-permute-start.14) | collective-permute-done | bytes 1572896 | tf_op jit(solution)/shard_map/ppermute | solution.py:46
  303.8 1.5 collective-permute-start.12
  305.2 8.9 %fusion.42 = f32[1024,2304]{1,0:T(8,128)} fusion(bf16[1024,1152]{1,0:T(8,128)(2,1)S(1)} %bitcast.83, bf16[2304,1152]{1,0:T(8,128)(2,1)S(1)} %bitcast.93), kind=kOutput, calls=%fused_computation.66 | convolution fusion | flops 5435817984 | bytes 17104896 | tf_op jit(solution)/shard_map/dot_general | solution.py:105
  314.2 23.3 %collective-permute-done.15 = bf16[1024,768]{1,0:T(8,128)(2,1)S(1)} collective-permute-done((bf16[1024,768]{1,0:T(8,128)(2,1)}, bf16[1024,768]{1,0:T(8,128)(2,1)S(1)}, u32[]{:S(2)}, u32[]{:S(2)}) %collective-permute-start.15) | collective-permute-done | bytes 1572896 | tf_op jit(solution)/shard_map/ppermute | solution.py:46
  337.5 1.2 copy-done.3
  338.6 31.7 %collective-permute-done.16 = bf16[1024,768]{1,0:T(8,128)(2,1)S(1)} collective-permute-done((bf16[1024,768]{1,0:T(8,128)(2,1)S(1)}, bf16[1024,768]{1,0:T(8,128)(2,1)S(1)}, u32[]{:S(2)}, u32[]{:S(2)}) %collective-permute-start.16) | collective-permute-done | bytes 1572896 | tf_op jit(solution)/shard_map/ppermute | solution.py:46
  371.5 12.7 %add_convert_fusion = bf16[1024,2304]{1,0:T(8,128)(2,1)} fusion(f32[1024,2304]{1,0:T(8,128)} %fusion.42, bf16[1024,768]{1,0:T(8,128)(2,1)} %copy-done.4, bf16[1024,768]{1,0:T(8,128)(2,1)} %copy-done.3, bf16[1024,768]{1,0:T(8,128)(2,1)} %copy-done.2, bf16[1024,1152]{1,0:T(8,128)(2,1)S(1)} %bitcast.82, bf16[2304,1152]{1,0:T(8,128)(2,1)} %collective-permute-done.13), kind=kOutput, calls=%fused_computation.4 | convolution fusion | flops 5457051648 | bytes 26542080 | tf_op jit(solution)/shard_map/dot_general | solution.py:105
  384.2 7.0 %collective-permute-done.12 = bf16[768,1152]{0,1:T(8,128)(2,1)} collective-permute-done((bf16[768,1152]{0,1:T(8,128)(2,1)}, bf16[768,1152]{0,1:T(8,128)(2,1)}, u32[]{:S(2)}, u32[]{:S(2)}) %collective-permute-start.12) | collective-permute-done | bytes 1769504 | tf_op jit(solution)/shard_map/ppermute | solution.py:50
  391.2 15.1 %fusion.1 = f32[2304,1152]{0,1:T(8,128)} fusion(f32[2304,1152]{0,1:T(8,128)} %convolution_bitcast_fusion.1, bf16[8,128,2304]{1,2,0:T(8,128)(2,1)} %collective-permute-done.7, bf16[768,1152]{0,1:T(8,128)(2,1)} %collective-permute-done.12, bf16[768,1152]{0,1:T(8,128)(2,1)} %collective-permute-done.11, bf16[768,1152]{0,1:T(8,128)(2,1)S(1)} %collective-permute-done.10, ...), kind=kOutput, calls=%fused_computation.2 | convolution fusion | flops 5460590592 | bytes 33620000 | tf_op jit(solution)/shard_map/dot_general | solution.py:93
  406.3 12.7 %copy.43 = f32[2304,1152]{1,0:T(8,128)} copy(f32[2304,1152]{0,1:T(8,128)} %fusion.1) | data formatting | bytes 21233664
  (52 shorter events, 8.0 us)
Async XLA Ops:
  7.2 181.9 %all-gather.2.cloned.1.call-start = ((), (), s32[]{:S(2)}) async-start(), calls=%async_computation.1 | async-start | bytes 10616832 | tf_op jit(solution)/shard_map/all_gather | solution.py:84
  8.6 17.6 %copy-start.1 = (bf16[8,16,4608]{2,1,0:T(8,128)(2,1)S(1)}, bf16[8,16,4608]{2,1,0:T(8,128)(2,1)}, u32[]{:S(2)}) copy-start(bf16[8,16,4608]{2,1,0:T(8,128)(2,1)} %param.5) | copy-start | bytes 3538948
  8.7 16.3 %collective-permute-start = (bf16[8,16,2304]{2,1,0:T(8,128)(2,1)S(1)}, bf16[8,16,2304]{2,1,0:T(8,128)(2,1)S(1)}, u32[]{:S(2)}, u32[]{:S(2)}) collective-permute-start(bf16[8,16,2304]{2,1,0:T(8,128)(2,1)S(1)} %pad_maximum_fusion.2), channel_id=1, source_target_pairs={{0,8},{8,0},{16,24},{24,16},{1,9},{9,1},{17,25},{25,17},{2,10},{10... | collective-permute-start | bytes 1769480 | tf_op jit(solution)/shard_map/ppermute | solution.py:46
  34.1 19.1 %copy-start.5 = (s32[8]{0:T(128)S(1)}, s32[8]{0:T(128)}, u32[]{:S(2)}) copy-start(s32[8]{0:T(128)} %param.7) | copy-start | bytes 100
  46.6 64.2 %all-to-all-start = ((bf16[8,2,36864]{2,1,0:T(2,128)(2,1)}), bf16[8,2,36864]{2,1,0:T(2,128)(2,1)S(1)}, u32[]{:S(2)}, u32[]{:S(2)}) async-start(bf16[8,2,36864]{2,1,0:T(2,128)(2,1)} %reshape.96), calls=%async_computation | async-start | bytes 2359296 | tf_op jit(solution)/shard_map/all_to_all | solution.py:75
  51.7 146.2 %collective-permute-start.13 = (bf16[2304,1152]{1,0:T(8,128)(2,1)}, bf16[2304,1152]{1,0:T(8,128)(2,1)}, u32[]{:S(2)}, u32[]{:S(2)}) collective-permute-start(bf16[2304,1152]{1,0:T(8,128)(2,1)} %param.6), channel_id=1, source_target_pairs={{0,16},{8,24},{16,0},{24,8},{1,17},{9,25},{17,1},{25,9},{2,18},{10... | collective-permute-start | bytes 15925256 | tf_op jit(solution)/shard_map/ppermute | solution.py:50
  128.5 2.0 collective-permute-start.1
  130.5 22.7 %collective-permute-start.2 = (f32[8,128,128]{2,1,0:T(8,128)S(1)}, f32[8,128,128]{2,1,0:T(8,128)S(1)}, u32[]{:S(2)}, u32[]{:S(2)}) collective-permute-start(f32[8,128,128]{2,1,0:T(8,128)S(1)} %add.108), channel_id=1, source_target_pairs={{0,2},{1,3},{2,0},{3,1},{4,6},{5,7},{6,4},{7,5},{8,10},{9,11},{10,... | collective-permute-start | bytes 1572872 | tf_op jit(solution)/shard_map/ppermute | solution.py:18
  130.6 27.9 %collective-permute-start.8 = (s32[8]{0:T(128)S(1)}, s32[8]{0:T(128)S(1)}, u32[]{:S(2)}, u32[]{:S(2)}) collective-permute-start(s32[8]{0:T(128)S(1)} %copy-done.5), channel_id=1, source_target_pairs={{0,8},{8,0},{16,24},{24,16},{1,9},{9,1},{17,25},{25,17},{2,10},{10... | collective-permute-start | bytes 104 | tf_op jit(solution)/shard_map/ppermute | solution.py:46
  153.3 25.0 %collective-permute-start.3 = (f32[8,128,128]{2,1,0:T(8,128)S(1)}, f32[8,128,128]{2,1,0:T(8,128)S(1)}, u32[]{:S(2)}, u32[]{:S(2)}) collective-permute-start(f32[8,128,128]{2,1,0:T(8,128)S(1)} %add.109), channel_id=1, source_target_pairs={{0,4},{1,5},{2,6},{3,7},{4,0},{5,1},{6,2},{7,3},{8,12},{9,13},{10,... | collective-permute-start | bytes 1572872 | tf_op jit(solution)/shard_map/ppermute | solution.py:18
  165.2 105.0 %collective-permute-start.7 = (bf16[8,128,2304]{1,2,0:T(8,128)(2,1)}, bf16[8,128,2304]{1,2,0:T(8,128)(2,1)}, u32[]{:S(2)}, u32[]{:S(2)}) collective-permute-start(bf16[8,128,2304]{1,2,0:T(8,128)(2,1)} %copy.35), channel_id=1, source_target_pairs={{0,8},{8,0},{16,24},{24,16},{1,9},{9,1},{17,25},{25,17},{2,10},{10... | collective-permute-start | bytes 14155784 | tf_op jit(solution)/shard_map/ppermute | solution.py:46
  178.5 1.2 collective-permute-start.4
  179.6 3.5 collective-permute-start.5
  183.2 4.4 %collective-permute-start.6 = (f32[8]{0:T(128)S(1)}, f32[8]{0:T(128)S(1)}, u32[]{:S(2)}, u32[]{:S(2)}) collective-permute-start(f32[8]{0:T(128)S(1)} %add.112), channel_id=1, source_target_pairs={{0,4},{1,5},{2,6},{3,7},{4,0},{5,1},{6,2},{7,3},{8,12},{9,13},{10,... | collective-permute-start | bytes 104 | tf_op jit(solution)/shard_map/ppermute | solution.py:18
  187.6 82.5 %collective-permute-start.9 = (f32[8]{0:T(128)S(1)}, f32[8]{0:T(128)S(1)}, u32[]{:S(2)}, u32[]{:S(2)}) collective-permute-start(f32[8]{0:T(128)S(1)} %rsqrt_multiply_fusion), channel_id=1, source_target_pairs={{0,8},{8,0},{16,24},{24,16},{1,9},{9,1},{17,25},{25,17},{2,10},{10... | collective-permute-start | bytes 104 | tf_op jit(solution)/shard_map/ppermute | solution.py:46
  189.1 5.9 %slice-start.2 = ((s8[5308416]{0:T(1024)(128)(4,1)}), s8[4194304]{0:T(1024)(128)(4,1)S(1)}, s32[]{:S(2)}) async-start(s8[5308416]{0:T(1024)(128)(4,1)} %bitcast.92), calls=%async_computation.4 | async-start | bytes 8388608
  193.4 94.5 %copy-start = (bf16[8,128,2304]{2,1,0:T(8,128)(2,1)}, bf16[8,128,2304]{2,1,0:T(8,128)(2,1)S(1)}, u32[]{:S(2)}) copy-start(bf16[8,128,2304]{2,1,0:T(8,128)(2,1)S(1)} %get-tuple-element.14) | copy-start | bytes 14155780
  193.4 2.2 slice-start.3
  205.1 98.7 %collective-permute-start.14 = (bf16[1024,768]{1,0:T(8,128)(2,1)}, bf16[1024,768]{1,0:T(8,128)(2,1)S(1)}, u32[]{:S(2)}, u32[]{:S(2)}) collective-permute-start(bf16[1024,768]{1,0:T(8,128)(2,1)} %add_convert_fusion.3), channel_id=1, source_target_pairs={{0,8},{8,0},{16,24},{24,16},{1,9},{9,1},{17,25},{25,17},{2,10},{10... | collective-permute-start | bytes 4718600 | tf_op jit(solution)/shard_map/ppermute | solution.py:46
  210.5 126.9 %collective-permute-start.15 = (bf16[1024,768]{1,0:T(8,128)(2,1)}, bf16[1024,768]{1,0:T(8,128)(2,1)S(1)}, u32[]{:S(2)}, u32[]{:S(2)}) collective-permute-start(bf16[1024,768]{1,0:T(8,128)(2,1)} %add_convert_fusion.2), channel_id=1, source_target_pairs={{0,8},{8,0},{16,24},{24,16},{1,9},{9,1},{17,25},{25,17},{2,10},{10... | collective-permute-start | bytes 4718600 | tf_op jit(solution)/shard_map/ppermute | solution.py:46
  212.0 6.7 %slice-start = ((s8[4718592]{0:T(1024)(128)(4,1)}), s8[4194304]{0:T(1024)(128)(4,1)S(1)}, s32[]{:S(2)}) async-start(s8[4718592]{0:T(1024)(128)(4,1)} %bitcast.78), calls=%async_computation.2 | async-start | bytes 8388608
  214.2 4.4 %slice-start.1 = ((s8[4718592]{0:T(1024)(128)(4,1)}), s8[524288]{0:T(1024)(128)(4,1)S(1)}, s32[]{:S(2)}) async-start(s8[4718592]{0:T(1024)(128)(4,1)} %bitcast.78), calls=%async_computation.3 | async-start | bytes 1048576
  218.0 152.3 %collective-permute-start.16 = (bf16[1024,768]{1,0:T(8,128)(2,1)S(1)}, bf16[1024,768]{1,0:T(8,128)(2,1)S(1)}, u32[]{:S(2)}, u32[]{:S(2)}) collective-permute-start(bf16[1024,768]{1,0:T(8,128)(2,1)S(1)} %add_convert_fusion.1), channel_id=1, source_target_pairs={{0,8},{8,0},{16,24},{24,16},{1,9},{9,1},{17,25},{25,17},{2,10},{10... | collective-permute-start | bytes 4718600 | tf_op jit(solution)/shard_map/ppermute | solution.py:46
  276.1 108.2 %collective-permute-start.10 = (bf16[768,1152]{0,1:T(8,128)(2,1)}, bf16[768,1152]{0,1:T(8,128)(2,1)S(1)}, u32[]{:S(2)}, u32[]{:S(2)}) collective-permute-start(bf16[768,1152]{0,1:T(8,128)(2,1)} %fusion.7), channel_id=1, source_target_pairs={{0,16},{8,24},{16,0},{24,8},{1,17},{9,25},{17,1},{25,9},{2,18},{10... | collective-permute-start | bytes 5308424 | tf_op jit(solution)/shard_map/ppermute | solution.py:50
  283.4 100.8 %collective-permute-start.11 = (bf16[768,1152]{0,1:T(8,128)(2,1)}, bf16[768,1152]{0,1:T(8,128)(2,1)}, u32[]{:S(2)}, u32[]{:S(2)}) collective-permute-start(bf16[768,1152]{0,1:T(8,128)(2,1)} %fusion.8), channel_id=1, source_target_pairs={{0,16},{8,24},{16,0},{24,8},{1,17},{9,25},{17,1},{25,9},{2,18},{10... | collective-permute-start | bytes 5308424 | tf_op jit(solution)/shard_map/ppermute | solution.py:50
  303.8 10.4 %copy-start.2 = (bf16[1024,768]{1,0:T(8,128)(2,1)}, bf16[1024,768]{1,0:T(8,128)(2,1)S(1)}, u32[]{:S(2)}) copy-start(bf16[1024,768]{1,0:T(8,128)(2,1)S(1)} %collective-permute-done.14) | copy-start | bytes 4718596
  303.8 87.5 %collective-permute-start.12 = (bf16[768,1152]{0,1:T(8,128)(2,1)}, bf16[768,1152]{0,1:T(8,128)(2,1)}, u32[]{:S(2)}, u32[]{:S(2)}) collective-permute-start(bf16[768,1152]{0,1:T(8,128)(2,1)} %fusion.9), channel_id=1, source_target_pairs={{0,16},{8,24},{16,0},{24,8},{1,17},{9,25},{17,1},{25,9},{2,18},{10... | collective-permute-start | bytes 5308424 | tf_op jit(solution)/shard_map/ppermute | solution.py:50
  337.5 1.2 copy-start.3
  370.4 1.1 copy-start.4
Sparse Core Ops, SparseCore 0:
  26.3 117.3 all-gather.1

commit v2 on v1

--- a/solution.py
+++ b/solution.py
@@ -1,8 +1,12 @@
+import functools
 import math
 
 import jax
 import jax.numpy as jnp
 from jax import lax
+from jax.experimental import pallas as pl
+from jax.experimental.layout import Layout, with_layout_constraint
+from jax.experimental.pallas import tpu as pltpu
 from jax.sharding import PartitionSpec as P
 
 F32 = jnp.float32
@@ -27,6 +31,197 @@
             break
     size = extent // count
     return [(i * size, (i + 1) * size) for i in range(count)]
+
+
+def exchange_kernel(ranks, cot, hid, w, whole, hid_in, w_in, prod, hid_v, cot_v, gram_h, gram_out, gram_in,
+                    local_sem, x_send, x_recv, big_send, big_recv, line_send, line_recv, core_send, core_recv,
+                    gram_send, gram_recv, load_sem):
+    seqs, chunk, _ = cot.shape
+    share = w.shape[1]
+    line = ranks // 2
+    dp, mp = lax.axis_index("dp"), lax.axis_index("mp")
+    row, col = dp // 2, dp % 2
+    place, core = mp // 2, mp % 2
+    across = {"dp": row * 2 + (1 - col)}
+    along = {"dp": (1 - row) * 2 + col}
+    sibling = {"mp": place * 2 + (1 - core)}
+    right, left = {"mp": mp + 2}, {"mp": mp - 2}
+    has_right, has_left = place < line - 1, place > 0
+
+    barrier = pltpu.get_barrier_semaphore()
+    for device in (across, along, sibling):
+        pl.semaphore_signal(barrier, inc=1, device_id=device, device_id_type=pl.DeviceIdType.MESH)
+
+    @pl.when(has_right)
+    def _():
+        pl.semaphore_signal(barrier, inc=1, device_id=right, device_id_type=pl.DeviceIdType.MESH)
+
+    @pl.when(has_left)
+    def _():
+        pl.semaphore_signal(barrier, inc=1, device_id=left, device_id_type=pl.DeviceIdType.MESH)
+
+    pl.semaphore_wait(barrier, 3 + jnp.where(has_right, 1, 0) + jnp.where(has_left, 1, 0))
+
+    def remote(src, dst, send, recv, device):
+        return pltpu.make_async_remote_copy(
+            src_ref=src, dst_ref=dst, send_sem=send, recv_sem=recv, device_id=device,
+            device_id_type=pl.DeviceIdType.MESH)
+
+    def slot(k, at, kore):
+        rows = pl.ds(pl.multiple_of((at * 2 + kore) * chunk, chunk), chunk)
+        return whole.at[pl.ds(k * seqs, seqs), rows, :]
+
+    def columns(m, c):
+        start = pl.multiple_of(((row + m) % 2 * 2 + c) * share, share)
+        return cot.at[:, :, pl.ds(start, share)]
+
+    def target(k, m):
+        rows = pl.ds(pl.multiple_of(mp * chunk, chunk), chunk)
+        return whole.at[pl.ds(k * seqs, seqs), rows, pl.ds(m * share, share)]
+
+    own = [pltpu.make_async_copy(columns(m, col), target(0, m), local_sem.at[m]) for m in range(2)]
+    over = [remote(columns(m, 1 - col), target(1, m), x_send.at[m], x_recv.at[m], across) for m in range(2)]
+    big = [remote(w, w_in, big_send.at[0], big_recv.at[0], along),
+           remote(hid, hid_in, big_send.at[1], big_recv.at[1], across)]
+    load_h = pltpu.make_async_copy(hid, hid_v, load_sem.at[0])
+    for copy in (*own, *over, *big, load_h):
+        copy.start()
+
+    def to_right(k, s):
+        return remote(slot(k, place - s, core), slot(k, place - s, core),
+                      line_send.at[k, 0, s], line_recv.at[k, 0, s], right)
+
+    def to_left(k, s):
+        return remote(slot(k, place + s, core), slot(k, place + s, core),
+                      line_send.at[k, 1, s], line_recv.at[k, 1, s], left)
+
+    def to_core(k, at):
+        return remote(slot(k, at, core), slot(k, at, core),
+                      core_send.at[k, at], core_recv.at[k, at], sibling)
+
+    def gram(ref, b):
+        value = ref[b]
+        return lax.dot_general(value, value, (((1,), (1,)), ((), ())), preferred_element_type=F32)
+
+    for k in range(2):
+        for copy in (own if k == 0 else over):
+            copy.wait()
+
+        @pl.when(has_right)
+        def _(k=k):
+            to_right(k, 0).start()
+
+        @pl.when(has_left)
+        def _(k=k):
+            to_left(k, 0).start()
+
+        to_core(k, place).start()
+        if k == 0:
+            continue
+        load_h.wait()
+
+        @pl.loop(0, seqs)
+        def _(b):
+            gram_h[b] = gram(hid_v, b)
+
+    for s in range(1, line):
+        for k in range(2):
+            @pl.when(place - s >= 0)
+            def _(k=k, s=s):
+                remote(slot(k, place - s, core), slot(k, place - s, core),
+                       line_send.at[k, 0, s - 1], line_recv.at[k, 0, s - 1], right).wait_recv()
+
+                @pl.when(has_right)
+                def _():
+                    to_right(k, s).start()
+
+                to_core(k, place - s).start()
+
+            @pl.when(place + s < line)
+            def _(k=k, s=s):
+                remote(slot(k, place + s, core), slot(k, place + s, core),
+                       line_send.at[k, 1, s - 1], line_recv.at[k, 1, s - 1], left).wait_recv()
+
+                @pl.when(has_left)
+                def _():
+                    to_left(k, s).start()
+
+                to_core(k, place + s).start()
+
+    def arrive(k):
+        for at in range(line):
+            remote(slot(k, at, 1 - core), slot(k, at, 1 - core),
+                   core_send.at[k, at], core_recv.at[k, at], sibling).wait_recv()
+        load = pltpu.make_async_copy(whole.at[pl.ds(k * seqs, seqs)], cot_v, load_sem.at[1])
+        load.start()
+        load.wait()
+
+    arrive(1)
+
+    @pl.loop(0, seqs)
+    def _(b):
+        gram_out[b] = gram(cot_v, b)
+
+    sums = remote(gram_out, gram_in, gram_send, gram_recv, across)
+    sums.start()
+    arrive(0)
+    sums.wait_recv()
+
+    @pl.loop(0, seqs)
+    def _(b):
+        gram_h[b] = gram_h[b] * (gram(cot_v, b) + gram_in[b])
+
+    result = pltpu.make_async_copy(gram_h, prod, load_sem.at[2])
+    result.start()
+    sums.wait_send()
+    for k in range(2):
+        for at in range(line):
+            to_core(k, at).wait_send()
+        for s in range(line - 1):
+            @pl.when(has_right & (place - s >= 0))
+            def _(k=k, s=s):
+                to_right(k, s).wait_send()
+
+            @pl.when(has_left & (place + s < line))
+            def _(k=k, s=s):
+                to_left(k, s).wait_send()
+    result.wait()
+    for copy in big:
+        copy.wait()
+
+
+def exchange(cotangent, hidden, w_down):
+    seqs, chunk, _ = cotangent.shape
+    ranks = lax.axis_size("mp")
+    share = w_down.shape[1]
+    line = ranks // 2
+    seq_len = chunk * ranks
+    dma = pltpu.SemaphoreType.DMA
+    square = (seqs, seq_len, seq_len)
+    anywhere = pl.BlockSpec(memory_space=pl.ANY)
+    return pl.pallas_call(
+        functools.partial(exchange_kernel, ranks),
+        out_shape=(
+            jax.ShapeDtypeStruct((2 * seqs, seq_len, 2 * share), BF16),
+            jax.ShapeDtypeStruct(hidden.shape, BF16),
+            jax.ShapeDtypeStruct(w_down.shape, BF16),
+            jax.ShapeDtypeStruct(square, F32),
+        ),
+        in_specs=[anywhere] * 3,
+        out_specs=(anywhere,) * 4,
+        scratch_shapes=[
+            pltpu.VMEM(hidden.shape, BF16),
+            pltpu.VMEM((seqs, seq_len, 2 * share), BF16),
+            pltpu.VMEM(square, F32),
+            pltpu.VMEM(square, F32),
+            pltpu.VMEM(square, F32),
+            dma((2,)), dma((2,)), dma((2,)), dma((2,)), dma((2,)),
+            dma((2, 2, line)), dma((2, 2, line)), dma((2, line)), dma((2, line)),
+            dma, dma, dma((3,)),
+        ],
+        compiler_params=pltpu.CompilerParams(
+            collective_id=0, has_side_effects=True, vmem_limit_bytes=48 * 1024 * 1024),
+    )(cotangent, hidden, w_down)
 
 
 def body(hidden, cotangent, w_down, lengths):
@@ -49,20 +244,6 @@
         perm = [(r * inner + c, (r + m) % outer * inner + c) for r in range(outer) for c in range(inner)]
         return lax.ppermute(value, "dp", perm)
 
-    def columns_of(c):
-        blocks = [
-            lax.dynamic_slice_in_dim(cotangent, ((row - m) % outer * inner + c) * share, share, 2)
-            for m in range(outer)
-        ]
-        return jnp.concatenate(blocks, axis=2)
-
-    cot_parts = [columns_of(col)]
-    for k in range(1, inner):
-        cot_parts.append(along_inner(columns_of((col + k) % inner), k))
-    held, *cot_parts = lax.optimization_barrier((hidden, *cot_parts))
-
-    w_parts = [w_down] + [along_outer(w_down, m) for m in range(1, outer)]
-    hid_parts = [hidden] + [along_inner(held, k) for k in range(1, inner)]
     len_parts = [lengths] + [along_inner(lengths, k) for k in range(1, inner)]
 
     positions = jnp.arange(seq_len, dtype=jnp.int32)
@@ -72,16 +253,37 @@
 
     keeps = [positions[None, :] < n[:, None] for n in len_parts]
 
-    slim = lax.all_to_all(cotangent, "mp", split_axis=2, concat_axis=1, tiled=True)
-    slim = masked_by(slim, keeps[0])
-    cot_gram = total_over(jnp.einsum("bsd,btd->bst", slim, slim, preferred_element_type=F32), "mp")
-    hid_gram = jnp.einsum("bsf,btf->bst", hidden, hidden, preferred_element_type=F32)
-    sq_norm = total_over(jnp.sum(hid_gram * cot_gram, axis=(1, 2)), "mp")
+    if (inner, outer) == (2, 2) and ranks % 2 == 0 and chunk % 16 == 0 and share % 128 == 0:
+        whole, hid_in, w_in, prod = exchange(cotangent, hidden, w_down)
+        whole = whole.reshape(inner, seqs, seq_len, inner * share)
+        w_parts, hid_parts = [w_down, w_in], [hidden, hid_in]
+        both = keeps[0][:, :, None] & keeps[0][:, None, :]
+        sq_norm = total_over(jnp.sum(jnp.where(both, prod, 0.0), axis=(1, 2)), "mp")
+    else:
+        def columns_of(c):
+            blocks = [
+                lax.dynamic_slice_in_dim(cotangent, ((row - m) % outer * inner + c) * share, share, 2)
+                for m in range(outer)
+            ]
+            return jnp.concatenate(blocks, axis=2)
+
+        cot_parts = [columns_of(col)]
+        for k in range(1, inner):
+            cot_parts.append(along_inner(columns_of((col + k) % inner), k))
+        held, *cot_parts = lax.optimization_barrier((hidden, *cot_parts))
+
+        w_parts = [w_down] + [along_outer(w_down, m) for m in range(1, outer)]
+        hid_parts = [hidden] + [along_inner(held, k) for k in range(1, inner)]
+        slim = lax.all_to_all(cotangent, "mp", split_axis=2, concat_axis=1, tiled=True)
+        slim = masked_by(slim, keeps[0])
+        cot_gram = total_over(jnp.einsum("bsd,btd->bst", slim, slim, preferred_element_type=F32), "mp")
+        hid_gram = jnp.einsum("bsf,btf->bst", hidden, hidden, preferred_element_type=F32)
+        sq_norm = total_over(jnp.sum(hid_gram * cot_gram, axis=(1, 2)), "mp")
+        whole = lax.all_gather(jnp.stack(cot_parts), "mp", axis=2, tiled=True)
     radius = math.sqrt(units * ranks * width / (seqs * groups))
     clip = radius / jnp.sqrt(sq_norm + 1e-06)
     clips = [clip] + [along_inner(clip, k) for k in range(1, inner)]
 
-    whole = lax.all_gather(jnp.stack(cot_parts), "mp", axis=2, tiled=True)
     masked = [masked_by(whole[k], keeps[k]) for k in range(inner)]
     tokens = seqs * seq_len
 
@@ -115,7 +317,8 @@
     grad_w_in = [[along_outer(grad_w(m, *cut).astype(BF16), -m) for m in range(1, outer)] for cut in cuts]
     grad_h_in = [[along_inner(grad_h(k, *cut).astype(BF16), -k) for k in range(1, inner)] for cut in cuts]
 
-    own_w, own_h = grad_w(0, 0, units), grad_h(0, 0, units)
+    own_w, own_h = lax.optimization_barrier((grad_w(0, 0, units), grad_h(0, 0, units)))
+    own_w = with_layout_constraint(own_w, Layout(major_to_minor=(0, 1)))
     for k in range(inner - 1):
         own_h = own_h + jnp.concatenate([parts[k] for parts in grad_h_in], axis=1).astype(F32)
     for m in range(outer - 1):

time: 433 us -> 390 us (0.901); the launches traced: 426 us -> 390 us
  Pallas kernels: 0 us -> 130 us
  waiting for transfers between devices: 221 us -> 138 us
  local copies, waits for them, and re-layouts: 62.2 us -> 2.68 us
  matrix products: 101 us -> 85.5 us
  between operations: 14.7 us -> 0.79 us
  other arithmetic: 6.31 us -> 17.3 us
  starting transfers between devices: 20.9 us -> 14.9 us
    pallas_call x0 -> x1, Pallas kernels: none -> 130 us  [exchange(): pl.pallas_call(functools.partial(exchange_kernel, ranks), out_shape=(jax....]
    ppermute x4 -> x3, waiting for transfers between devices: 7.01 us -> 87.6 us  [along_outer(): return lax.ppermute(value, 'dp', perm)]
    ppermute x7 -> x5, waiting for transfers between devices: 113 us -> 48.8 us  [along_inner(): return lax.ppermute(value, 'dp', perm)]
    all_to_all x1 -> x0, waiting for transfers between devices: 57.5 us -> none  [body(): lax.all_to_all(cotangent, 'mp', split_axis=2, concat_axis=1, tiled=True)]
    unnamed x24 -> x20, local copies, waits for them, and re-layouts: 44 us -> 1.89 us
    ppermute x6 -> x3, waiting for transfers between devices: 43.4 us -> 1.93 us  [total_over(): lax.ppermute(value, axis, [(i, i ^ step) for i in range(size)])]
    dot_general x8, matrix products: 53.1 us -> 41.6 us  [grad_w(): lax.dot_general(hid_parts[k][:, :, lo:hi].reshape(tokens, hi - lo), scale...]
    all_to_all x1 -> x0, local copies, waits for them, and re-layouts: 8.75 us -> none  [body(): lax.all_to_all(cotangent, 'mp', split_axis=2, concat_axis=1, tiled=True)]
  transfers between devices with their start and end apart: 19 -> 11, of which waited for: 13 -> 5; matrix products, arithmetic and copies ran while one was open for 32% -> 25% of each run, Pallas kernels for 0% -> 33%
where the time goes in v2:
time: 390 us
  waiting for transfers between devices  138 us (35%)
  Pallas kernels  130 us (33%)
  matrix products  85.5 us (22%)
  other arithmetic  17.3 us (4%)
  starting transfers between devices  14.9 us (4%)
    pallas_call x1, Pallas kernels, exchange(): pl.pallas_call(functools.partial(exchange_kernel, ranks), out_shape=(jax....  130 us
    ppermute x3, waiting for transfers between devices, along_outer(): return lax.ppermute(value, 'dp', perm)  87.6 us
    ppermute x5, waiting for transfers between devices, along_inner(): return lax.ppermute(value, 'dp', perm)  48.8 us
    dot_general x8, matrix products, grad_h(): lax.dot_general(masked[k][:, :, m * share:(m + 1) * share].reshape(tokens...  43.9 us
    dot_general x8, matrix products, grad_w(): lax.dot_general(hid_parts[k][:, :, lo:hi].reshape(tokens, hi - lo), scale...  41.6 us
  transfers between devices with their start and end apart: 11, of which 5 were waited for; matrix products, arithmetic and copies ran while one was open for 25% of the time, Pallas kernels for 33%

profile of v2, /device:TPU:0, one launch (start us, length us, event | category | flops | bytes accessed | tf_op | source)
XLA Modules:
  0.0 389.9 jit_solution(14649613277606641815)
XLA Ops:
  0.6 3.0 collective-permute-start.3
  3.6 0.8 iota_compare_fusion.1
  4.4 1.3 copy-done
  5.7 130.4 %shard_map.59 = (bf16[16,128,2304]{2,1,0:T(8,128)(2,1)}, bf16[8,128,2304]{2,1,0:T(8,128)(2,1)}, bf16[2304,1152]{1,0:T(8,128)(2,1)}, f32[8,128,128]{2,1,0:T(8,128)S(1)}) custom-call(bf16[8,16,4608]{2,1,0:T(8,128)(2,1)S(1)} %copy-done, bf16[8,128,2304]{2,1,0:T(8,128)(2,1)} %hid.1, bf16[2304,1152]{1,0:T(8,128)(2,1)} %w.1), custom_call_target="tpu_custom_call" | custom-call | tf_op jit(solution)/shard_map/pallas_call | solution.py:202
  136.1 0.3 select_reduce_fusion
  136.4 0.1 collective-permute-start
  136.4 0.0 collective-permute-done.3
  136.5 0.1 iota_compare_fusion
  136.5 4.3 %slice_select_fusion = (bf16[8,128,2304]{2,1,0:T(8,128)(2,1)S(1)}, bf16[8,128,2304]{2,1,0:T(8,128)(2,1)S(1)}) fusion(bf16[16,128,2304]{2,1,0:T(8,128)(2,1)} %get-tuple-element.8, pred[8,128]{1,0:T(8,128)(4,1)S(1)} %iota_compare_fusion, pred[8,128]{1,0:T(8,128)(4,1)S(1)} %iota_compare_fusion.1), kind=kLoop, calls=%fused_computation.9 | loop fusion | flops 4718592 | bytes 18876416 | tf_op jit(solution)/shard_map/jit(_where)/select_n | solution.py:252
  140.9 0.0 slice-start.5
  140.9 0.8 fusion.35
  141.7 0.6 slice-done.5
  142.3 3.9 %fusion.9 = f32[1024,768]{1,0:T(8,128)} fusion(bf16[1024,1152]{1,0:T(8,128)(2,1)S(1)} %bitcast.65, bf16[2304,1152]{1,0:T(8,128)(2,1)S(1)} %bitcast.69), kind=kOutput, calls=%fused_computation.29 | convolution fusion | flops 1811939328 | bytes 7274496 | tf_op jit(solution)/shard_map/dot_general | solution.py:307
  146.2 3.9 %fusion.13 = f32[1024,768]{1,0:T(8,128)} fusion(bf16[1024,1152]{1,0:T(8,128)(2,1)S(1)} %bitcast.66, bf16[2304,1152]{1,0:T(8,128)(2,1)S(1)} %bitcast.69), kind=kOutput, calls=%fused_computation.33 | convolution fusion | flops 1811939328 | bytes 7274496 | tf_op jit(solution)/shard_map/dot_general | solution.py:307
  150.1 2.2 fusion.17
  152.3 0.0 collective-permute-done
  152.4 1.7 collective-permute-start.1
  154.1 5.5 %add_convert_fusion.1 = bf16[1024,768]{1,0:T(8,128)(2,1)} fusion(f32[1024,768]{1,0:T(8,128)} %fusion.9, bf16[1024,1152]{1,0:T(8,128)(2,1)S(1)} %bitcast.62, bf16[2304,1152]{1,0:T(8,128)(2,1)S(1)} %bitcast.56), kind=kOutput, calls=%fused_computation.24 | convolution fusion | flops 1813512192 | bytes 8847360 | tf_op jit(solution)/shard_map/dot_general | solution.py:307
  159.6 1.4 collective-permute-start.10
  161.0 3.4 add_convert_fusion.2
  164.5 3.5 add_convert_fusion.3
  167.9 0.6 collective-permute-start.8
  168.5 1.4 collective-permute-start.9
  169.9 8.7 %fusion.37 = f32[1024,2304]{1,0:T(8,128)} fusion(bf16[1024,1152]{1,0:T(8,128)(2,1)S(1)} %bitcast.61, bf16[2304,1152]{1,0:T(8,128)(2,1)S(1)} %bitcast.56), kind=kOutput, calls=%fused_computation.55 | convolution fusion | flops 5435817984 | bytes 17104896 | tf_op jit(solution)/shard_map/dot_general | solution.py:307
  178.6 12.8 %convolution_add_fusion = f32[1024,2304]{1,0:T(8,128)} fusion(f32[1024,2304]{1,0:T(8,128)} %fusion.37, bf16[1024,1152]{1,0:T(8,128)(2,1)S(1)} %bitcast.60, bf16[2304,1152]{1,0:T(8,128)(2,1)} %get-tuple-element.11), kind=kOutput, calls=%fused_computation.5 | convolution fusion | flops 5438177280 | bytes 26542080 | tf_op jit(solution)/shard_map/dot_general | solution.py:307
  191.4 0.0 collective-permute-done.1
  191.4 2.6 collective-permute-start.2
  194.0 1.9 collective-permute-done.2
  195.9 0.6 collective-permute-start.4
  196.5 4.1 %convolution_bitcast_fusion.5 = f32[768,1152]{1,0:T(8,128)} fusion(bf16[8,128,2304]{2,1,0:T(8,128)(2,1)S(1)} %bitcast.58, f32[8]{0:T(128)S(1)} %rsqrt_multiply_fusion, bf16[8,128,2304]{2,1,0:T(8,128)(2,1)S(1)} %get-tuple-element.15), kind=kOutput, calls=%fused_computation.17 | convolution fusion | flops 1815478272 | bytes 7471616 | tf_op jit(solution)/shard_map/dot_general | solution.py:295
  200.7 2.4 convolution_bitcast_fusion.3
  203.1 0.0 slice-start.6
  203.1 2.4 convolution_bitcast_fusion.7
  205.6 0.0 slice-start.7
  205.6 9.4 %convolution_bitcast_fusion.1 = f32[2304,1152]{1,0:T(8,128)} fusion(bf16[8,128,2304]{2,1,0:T(8,128)(2,1)S(1)} %bitcast.58, f32[8]{0:T(128)S(1)} %rsqrt_multiply_fusion, bf16[8,128,2304]{2,1,0:T(8,128)(2,1)S(1)} %get-tuple-element.15), kind=kOutput, calls=%fused_computation.2 | convolution fusion | flops 5439356928 | bytes 17695232 | tf_op jit(solution)/shard_map/dot_general | solution.py:295
  215.0 48.8 %collective-permute-done.4 = f32[8]{0:T(128)S(1)} collective-permute-done((f32[8]{0:T(128)S(1)}, f32[8]{0:T(128)S(1)}, u32[]{:S(2)}, u32[]{:S(2)}) %collective-permute-start.4) | collective-permute-done | bytes 64 | tf_op jit(solution)/shard_map/ppermute | solution.py:241
  263.9 5.7 %fusion.5 = bf16[768,1152]{1,0:T(8,128)(2,1)} fusion(f32[768,1152]{1,0:T(8,128)} %convolution_bitcast_fusion.5, bf16[8,128,2304]{2,1,0:T(8,128)(2,1)S(1)} %bitcast.71, f32[8]{0:T(128)S(1)} %collective-permute-done.4, bf16[8,128,2304]{2,1,0:T(8,128)(2,1)S(1)} %get-tuple-element.14), kind=kOutput, calls=%fused_computation.22 | convolution fusion | flops 1817247744 | bytes 9241088 | tf_op jit(solution)/shard_map/dot_general | solution.py:295
  269.6 1.5 collective-permute-start.6
  271.0 3.7 fusion.6
  274.8 0.6 collective-permute-start.7
  275.3 3.7 fusion.4
  279.1 1.5 collective-permute-start.5
  280.5 10.0 %fusion = f32[2304,1152]{1,0:T(8,128)S(1)} fusion(f32[2304,1152]{1,0:T(8,128)} %convolution_bitcast_fusion.1, bf16[8,128,2304]{2,1,0:T(8,128)(2,1)} %get-tuple-element.10, f32[8]{0:T(128)S(1)} %collective-permute-done.4, bf16[8,128,2304]{2,1,0:T(8,128)(2,1)S(1)} %get-tuple-element.14), kind=kOutput, calls=%fused_computation.1 | convolution fusion | flops 5442011136 | bytes 28312064 | tf_op jit(solution)/shard_map/dot_general | solution.py:295
  290.5 7.4 %add_convert_fusion = bf16[1024,2304]{1,0:T(8,128)(2,1)} fusion(f32[1024,2304]{1,0:T(8,128)} %convolution_add_fusion, bf16[1024,768]{1,0:T(8,128)(2,1)S(1)} %collective-permute-done.10, bf16[1024,768]{1,0:T(8,128)(2,1)} %collective-permute-done.9, bf16[1024,768]{1,0:T(8,128)(2,1)} %collective-permute-done.8), kind=kLoop, calls=%fused_computation.4 | loop fusion | flops 18874368 | bytes 18874368 | tf_op jit(solution)/shard_map/convert_element_type | solution.py:326
  297.9 13.4 %collective-permute-done.6 = bf16[768,1152]{1,0:T(8,128)(2,1)S(1)} collective-permute-done((bf16[768,1152]{1,0:T(8,128)(2,1)}, bf16[768,1152]{1,0:T(8,128)(2,1)S(1)}, u32[]{:S(2)}, u32[]{:S(2)}) %collective-permute-start.6) | collective-permute-done | bytes 1769504 | tf_op jit(solution)/shard_map/ppermute | solution.py:245
  311.4 37.9 %collective-permute-done.7 = bf16[768,1152]{1,0:T(8,128)(2,1)S(1)} collective-permute-done((bf16[768,1152]{1,0:T(8,128)(2,1)}, bf16[768,1152]{1,0:T(8,128)(2,1)S(1)}, u32[]{:S(2)}, u32[]{:S(2)}) %collective-permute-start.7) | collective-permute-done | bytes 1769504 | tf_op jit(solution)/shard_map/ppermute | solution.py:245
  349.3 36.3 %collective-permute-done.5 = bf16[768,1152]{1,0:T(8,128)(2,1)S(1)} collective-permute-done((bf16[768,1152]{1,0:T(8,128)(2,1)}, bf16[768,1152]{1,0:T(8,128)(2,1)S(1)}, u32[]{:S(2)}, u32[]{:S(2)}) %collective-permute-start.5) | collective-permute-done | bytes 1769504 | tf_op jit(solution)/shard_map/ppermute | solution.py:245
  385.5 4.4 %convert_add_fusion = f32[2304,1152]{1,0:T(8,128)} fusion(f32[2304,1152]{1,0:T(8,128)S(1)} %fusion, bf16[768,1152]{1,0:T(8,128)(2,1)S(1)} %collective-permute-done.7, bf16[768,1152]{1,0:T(8,128)(2,1)S(1)} %collective-permute-done.6, bf16[768,1152]{1,0:T(8,128)(2,1)S(1)} %collective-permute-done.5), kind=kLoop, calls=%fused_computation.3 | loop fusion | flops 18579456 | bytes 26542080 | tf_op jit(solution)/shard_map/add | solution.py:325
  (25 shorter events, 0.1 us)
Async XLA Ops:
  0.6 135.8 %collective-permute-start.3 = (s32[8]{0:T(128)}, s32[8]{0:T(128)S(1)}, u32[]{:S(2)}, u32[]{:S(2)}) collective-permute-start(s32[8]{0:T(128)} %param.7), channel_id=1, source_target_pairs={{0,8},{8,0},{16,24},{24,16},{1,9},{9,1},{17,25},{25,17},{2,10},{10... | collective-permute-start | bytes 104 | tf_op jit(solution)/shard_map/ppermute | solution.py:241
  4.4 1.3 copy-start
  136.4 15.9 %collective-permute-start = (f32[8]{0:T(128)S(1)}, f32[8]{0:T(128)S(1)}, u32[]{:S(2)}, u32[]{:S(2)}) collective-permute-start(f32[8]{0:T(128)S(1)} %select_reduce_fusion), channel_id=1, source_target_pairs={{0,1},{1,0},{2,3},{3,2},{4,5},{5,4},{6,7},{7,6},{8,9},{9,8},{10,11... | collective-permute-start | bytes 104 | tf_op jit(solution)/shard_map/ppermute | solution.py:22
  136.5 5.1 %slice-start.4 = ((s8[5308416]{0:T(1024)(128)(4,1)}), s8[4194304]{0:T(1024)(128)(4,1)S(1)}, s32[]{:S(2)}) async-start(s8[5308416]{0:T(1024)(128)(4,1)} %bitcast.68), calls=%async_computation.4 | async-start | bytes 8388608
  140.9 1.4 slice-start.5
  146.2 7.9 %slice-start = ((s8[5308416]{0:T(1024)(128)(4,1)}), s8[4194304]{0:T(1024)(128)(4,1)S(1)}, s32[]{:S(2)}) async-start(s8[5308416]{0:T(1024)(128)(4,1)} %bitcast.55), calls=%async_computation | async-start | bytes 8388608
  150.1 4.0 %slice-start.1 = ((s8[5308416]{0:T(1024)(128)(4,1)}), s8[1114112]{0:T(1024)(128)(4,1)S(1)}, s32[]{:S(2)}) async-start(s8[5308416]{0:T(1024)(128)(4,1)} %bitcast.55), calls=%async_computation.1 | async-start | bytes 2228224
  152.4 39.0 %collective-permute-start.1 = (f32[8]{0:T(128)S(1)}, f32[8]{0:T(128)S(1)}, u32[]{:S(2)}, u32[]{:S(2)}) collective-permute-start(f32[8]{0:T(128)S(1)} %add.42), channel_id=1, source_target_pairs={{0,2},{1,3},{2,0},{3,1},{4,6},{5,7},{6,4},{7,5},{8,10},{9,11},{10,... | collective-permute-start | bytes 104 | tf_op jit(solution)/shard_map/ppermute | solution.py:22
  154.1 7.0 %copy-start.1 = (f32[1024,768]{1,0:T(8,128)S(1)}, f32[1024,768]{1,0:T(8,128)}, u32[]{:S(2)}) copy-start(f32[1024,768]{1,0:T(8,128)} %fusion.13) | copy-start | bytes 9437188
  159.6 119.5 %collective-permute-start.10 = (bf16[1024,768]{1,0:T(8,128)(2,1)}, bf16[1024,768]{1,0:T(8,128)(2,1)S(1)}, u32[]{:S(2)}, u32[]{:S(2)}) collective-permute-start(bf16[1024,768]{1,0:T(8,128)(2,1)} %add_convert_fusion.1), channel_id=1, source_target_pairs={{0,8},{8,0},{16,24},{24,16},{1,9},{9,1},{17,25},{25,17},{2,10},{10... | collective-permute-start | bytes 4718600 | tf_op jit(solution)/shard_map/ppermute | solution.py:241
  167.9 122.6 %collective-permute-start.8 = (bf16[1024,768]{1,0:T(8,128)(2,1)}, bf16[1024,768]{1,0:T(8,128)(2,1)}, u32[]{:S(2)}, u32[]{:S(2)}) collective-permute-start(bf16[1024,768]{1,0:T(8,128)(2,1)} %add_convert_fusion.3), channel_id=1, source_target_pairs={{0,8},{8,0},{16,24},{24,16},{1,9},{9,1},{17,25},{25,17},{2,10},{10... | collective-permute-start | bytes 4718600 | tf_op jit(solution)/shard_map/ppermute | solution.py:241
  168.5 122.0 %collective-permute-start.9 = (bf16[1024,768]{1,0:T(8,128)(2,1)}, bf16[1024,768]{1,0:T(8,128)(2,1)}, u32[]{:S(2)}, u32[]{:S(2)}) collective-permute-start(bf16[1024,768]{1,0:T(8,128)(2,1)} %add_convert_fusion.2), channel_id=1, source_target_pairs={{0,8},{8,0},{16,24},{24,16},{1,9},{9,1},{17,25},{25,17},{2,10},{10... | collective-permute-start | bytes 4718600 | tf_op jit(solution)/shard_map/ppermute | solution.py:241
  169.9 26.6 %slice-start.2 = ((s8[4718592]{0:T(1024)(128)(4,1)}), s8[4194304]{0:T(1024)(128)(4,1)S(1)}, s32[]{:S(2)}) async-start(s8[4718592]{0:T(1024)(128)(4,1)} %bitcast.57), calls=%async_computation.2 | async-start | bytes 8388608
  178.6 17.9 %slice-start.3 = ((s8[4718592]{0:T(1024)(128)(4,1)}), s8[524288]{0:T(1024)(128)(4,1)S(1)}, s32[]{:S(2)}) async-start(s8[4718592]{0:T(1024)(128)(4,1)} %bitcast.57), calls=%async_computation.3 | async-start | bytes 1048576
  191.4 4.5 %collective-permute-start.2 = (f32[8]{0:T(128)S(1)}, f32[8]{0:T(128)S(1)}, u32[]{:S(2)}, u32[]{:S(2)}) collective-permute-start(f32[8]{0:T(128)S(1)} %add.43), channel_id=1, source_target_pairs={{0,4},{1,5},{2,6},{3,7},{4,0},{5,1},{6,2},{7,3},{8,12},{9,13},{10,... | collective-permute-start | bytes 104 | tf_op jit(solution)/shard_map/ppermute | solution.py:22
  195.9 67.9 %collective-permute-start.4 = (f32[8]{0:T(128)S(1)}, f32[8]{0:T(128)S(1)}, u32[]{:S(2)}, u32[]{:S(2)}) collective-permute-start(f32[8]{0:T(128)S(1)} %rsqrt_multiply_fusion), channel_id=1, source_target_pairs={{0,8},{8,0},{16,24},{24,16},{1,9},{9,1},{17,25},{25,17},{2,10},{10... | collective-permute-start | bytes 104 | tf_op jit(solution)/shard_map/ppermute | solution.py:241
  203.1 60.7 %slice-start.6 = ((s8[4718592]{0:T(1024)(128)(4,1)}), s8[4194304]{0:T(1024)(128)(4,1)S(1)}, s32[]{:S(2)}) async-start(s8[4718592]{0:T(1024)(128)(4,1)} %bitcast.70), calls=%async_computation.6 | async-start | bytes 8388608
  205.6 58.3 %slice-start.7 = ((s8[4718592]{0:T(1024)(128)(4,1)}), s8[524288]{0:T(1024)(128)(4,1)S(1)}, s32[]{:S(2)}) async-start(s8[4718592]{0:T(1024)(128)(4,1)} %bitcast.70), calls=%async_computation.7 | async-start | bytes 1048576
  269.6 41.8 %collective-permute-start.6 = (bf16[768,1152]{1,0:T(8,128)(2,1)}, bf16[768,1152]{1,0:T(8,128)(2,1)S(1)}, u32[]{:S(2)}, u32[]{:S(2)}) collective-permute-start(bf16[768,1152]{1,0:T(8,128)(2,1)} %fusion.5), channel_id=1, source_target_pairs={{0,16},{8,24},{16,0},{24,8},{1,17},{9,25},{17,1},{25,9},{2,18},{10... | collective-permute-start | bytes 5308424 | tf_op jit(solution)/shard_map/ppermute | solution.py:245
  274.8 74.5 %collective-permute-start.7 = (bf16[768,1152]{1,0:T(8,128)(2,1)}, bf16[768,1152]{1,0:T(8,128)(2,1)S(1)}, u32[]{:S(2)}, u32[]{:S(2)}) collective-permute-start(bf16[768,1152]{1,0:T(8,128)(2,1)} %fusion.6), channel_id=1, source_target_pairs={{0,16},{8,24},{16,0},{24,8},{1,17},{9,25},{17,1},{25,9},{2,18},{10... | collective-permute-start | bytes 5308424 | tf_op jit(solution)/shard_map/ppermute | solution.py:245
  279.1 106.5 %collective-permute-start.5 = (bf16[768,1152]{1,0:T(8,128)(2,1)}, bf16[768,1152]{1,0:T(8,128)(2,1)S(1)}, u32[]{:S(2)}, u32[]{:S(2)}) collective-permute-start(bf16[768,1152]{1,0:T(8,128)(2,1)} %fusion.4), channel_id=1, source_target_pairs={{0,16},{8,24},{16,0},{24,8},{1,17},{9,25},{17,1},{25,9},{2,18},{10... | collective-permute-start | bytes 5308424 | tf_op jit(solution)/shard_map/ppermute | solution.py:245

commit v3 on v2

--- a/solution.py
+++ b/solution.py
@@ -284,6 +284,7 @@
     clip = radius / jnp.sqrt(sq_norm + 1e-06)
     clips = [clip] + [along_inner(clip, k) for k in range(1, inner)]
 
+    whole, *clips = lax.optimization_barrier((whole, *clips))
     masked = [masked_by(whole[k], keeps[k]) for k in range(inner)]
     tokens = seqs * seq_len
 
@@ -301,11 +302,11 @@
             total = term if total is None else total + term
         return total
 
-    def grad_h(k, lo, hi):
+    def grad_h(source, lo, hi):
         total = None
         for m in range(outer):
             term = lax.dot_general(
-                masked[k][:, :, m * share:(m + 1) * share].reshape(tokens, share),
+                source[:, :, m * share:(m + 1) * share].reshape(tokens, share),
                 w_parts[m][lo:hi],
                 (((1,), (1,)), ((), ())),
                 preferred_element_type=F32,
@@ -314,10 +315,14 @@
         return total
 
     cuts = pieces(units, 3)
-    grad_w_in = [[along_outer(grad_w(m, *cut).astype(BF16), -m) for m in range(1, outer)] for cut in cuts]
-    grad_h_in = [[along_inner(grad_h(k, *cut).astype(BF16), -k) for k in range(1, inner)] for cut in cuts]
-
-    own_w, own_h = lax.optimization_barrier((grad_w(0, 0, units), grad_h(0, 0, units)))
+    w_terms = [[grad_w(m, *cut).astype(BF16) for m in range(1, outer)] for cut in cuts]
+    grad_w_in = [[along_outer(terms[m - 1], -m) for m in range(1, outer)] for terms in w_terms]
+    others, w_terms[0] = lax.optimization_barrier((masked[1:], w_terms[0]))
+    grad_h_in = [
+        [along_inner(grad_h(others[k - 1], *cut).astype(BF16), -k) for k in range(1, inner)] for cut in cuts
+    ]
+
+    own_w, own_h = lax.optimization_barrier((grad_w(0, 0, units), grad_h(masked[0], 0, units)))
     own_w = with_layout_constraint(own_w, Layout(major_to_minor=(0, 1)))
     for k in range(inner - 1):
         own_h = own_h + jnp.concatenate([parts[k] for parts in grad_h_in], axis=1).astype(F32)

time: 390 us -> 317 us (0.81)
  waiting for transfers between devices: 138 us -> 57 us
  matrix products: 85.5 us -> 90.1 us
    ppermute x3, waiting for transfers between devices: 87.6 us -> 0.01 us  [along_outer(): return lax.ppermute(value, 'dp', perm)]
    dot_general x8, matrix products: 41.6 us -> 46.5 us  [grad_w(): lax.dot_general(hid_parts[k][:, :, lo:hi].reshape(tokens, hi - lo), scale...]
  transfers between devices with their start and end apart: 11 -> 11, of which waited for: 5 -> 7; matrix products, arithmetic and copies ran while one was open for 25% -> 28% of each run, Pallas kernels for 33% -> 41%
where the time goes in v3:
time: 317 us
  Pallas kernels  130 us (41%)
  matrix products  90.1 us (28%)
  waiting for transfers between devices  57 us (18%)
  other arithmetic  19.1 us (6%)
  starting transfers between devices  15.9 us (5%)
  local copies, waits for them, and re-layouts  3.52 us (1%)
    pallas_call x1, Pallas kernels, exchange(): pl.pallas_call(functools.partial(exchange_kernel, ranks), out_shape=(jax....  130 us
    ppermute x5, waiting for transfers between devices, along_inner(): return lax.ppermute(value, 'dp', perm)  52.2 us
    dot_general x8, matrix products, grad_w(): lax.dot_general(hid_parts[k][:, :, lo:hi].reshape(tokens, hi - lo), scale...  46.5 us
    dot_general x8, matrix products, grad_h(): lax.dot_general(source[:, :, m * share:(m + 1) * share].reshape(tokens, s...  43.6 us
    ppermute x5, starting transfers between devices, along_inner(): return lax.ppermute(value, 'dp', perm)  8.08 us
    convert_element_type x1, other arithmetic, body(): return (own_w, own_h.astype(BF16).reshape(seqs, seq_len, units))  7.84 us
  transfers between devices with their start and end apart: 11, of which 7 were waited for; matrix products, arithmetic and copies ran while one was open for 28% of the time, Pallas kernels for 41%

profile of v3, /device:TPU:0, one launch (start us, length us, event | category | flops | bytes accessed | tf_op | source)
XLA Modules:
  0.0 316.9 jit_solution(9017826460359903503)
XLA Ops:
  0.6 3.0 collective-permute-start.4
  3.6 0.8 iota_compare_fusion.1
  4.4 1.3 copy-done
  5.7 130.4 %shard_map.59 = (bf16[16,128,2304]{2,1,0:T(8,128)(2,1)}, bf16[8,128,2304]{2,1,0:T(8,128)(2,1)}, bf16[2304,1152]{1,0:T(8,128)(2,1)}, f32[8,128,128]{2,1,0:T(8,128)S(1)}) custom-call(bf16[8,16,4608]{2,1,0:T(8,128)(2,1)S(1)} %copy-done, bf16[8,128,2304]{2,1,0:T(8,128)(2,1)} %hid.1, bf16[2304,1152]{1,0:T(8,128)(2,1)} %w.1), custom_call_target="tpu_custom_call" | custom-call | tf_op jit(solution)/shard_map/pallas_call | solution.py:202
  136.1 0.0 slice-start.2
  136.1 0.3 select_reduce_fusion
  136.4 0.1 collective-permute-start
  136.5 1.1 collective-permute-done
  137.6 1.6 collective-permute-start.1
  139.2 0.1 iota_compare_fusion
  139.3 1.8 collective-permute-done.1
  141.1 2.6 collective-permute-start.2
  143.7 1.9 collective-permute-done.2
  145.6 1.5 collective-permute-start.3
  147.1 2.1 collective-permute-done.3
  149.1 4.2 %bitcast_select_fusion = (bf16[8,128,2304]{2,1,0:T(8,128)(2,1)S(1)}, bf16[8,128,2304]{2,1,0:T(8,128)(2,1)S(1)}) fusion(bf16[2,8,128,2304]{3,2,1,0:T(8,128)(2,1)} %bitcast.60, pred[8,128]{1,0:T(8,128)(4,1)S(1)} %iota_compare_fusion, pred[8,128]{1,0:T(8,128)(4,1)S(1)} %iota_compare_fusion.1), kind=kLoop, calls=%fused_computation.6 | loop fusion | flops 4718592 | bytes 18876416 | tf_op jit(solution)/shard_map/jit(_where)/select_n | solution.py:252
  153.4 4.2 %convolution_bitcast_fusion.3 = f32[768,1152]{1,0:T(8,128)} fusion(bf16[8,128,2304]{2,1,0:T(8,128)(2,1)S(1)} %bitcast.64, f32[8]{0:T(128)S(1)} %rsqrt_multiply_fusion, bf16[8,128,2304]{2,1,0:T(8,128)(2,1)S(1)} %get-tuple-element.23), kind=kOutput, calls=%fused_computation.14 | convolution fusion | flops 1815478272 | bytes 7471616 | tf_op jit(solution)/shard_map/dot_general | solution.py:296
  157.6 2.4 convolution_bitcast_fusion.7
  160.0 0.0 slice-start.4
  160.0 5.1 %fusion.4 = bf16[768,1152]{1,0:T(8,128)(2,1)} fusion(f32[768,1152]{1,0:T(8,128)S(1)} %convolution_bitcast_fusion.7, bf16[8,128,2304]{2,1,0:T(8,128)(2,1)} %get-tuple-element.16, bf16[8,128,2304]{2,1,0:T(8,128)(2,1)S(1)} %get-tuple-element.21, f32[8]{0:T(128)S(1)} %collective-permute-done.3), kind=kOutput, calls=%fused_computation.21 | convolution fusion | flops 1817247744 | bytes 9241088 | tf_op jit(solution)/shard_map/dot_general | solution.py:296
  165.1 1.5 collective-permute-start.5
  166.6 4.1 %convolution_bitcast_fusion.5 = f32[768,1152]{1,0:T(8,128)} fusion(bf16[8,128,2304]{2,1,0:T(8,128)(2,1)S(1)} %bitcast.64, f32[8]{0:T(128)S(1)} %rsqrt_multiply_fusion, bf16[8,128,2304]{2,1,0:T(8,128)(2,1)S(1)} %get-tuple-element.23), kind=kOutput, calls=%fused_computation.17 | convolution fusion | flops 1815478272 | bytes 7471616 | tf_op jit(solution)/shard_map/dot_general | solution.py:296
  170.7 0.4 fusion.35
  171.2 3.9 %fusion.10 = f32[1024,768]{1,0:T(8,128)} fusion(bf16[1024,1152]{1,0:T(8,128)(2,1)S(1)} %bitcast.71, bf16[2304,1152]{1,0:T(8,128)(2,1)S(1)} %bitcast.75), kind=kOutput, calls=%fused_computation.30 | convolution fusion | flops 1811939328 | bytes 7274496 | tf_op jit(solution)/shard_map/dot_general | solution.py:308
  175.1 3.9 %fusion.14 = f32[1024,768]{1,0:T(8,128)} fusion(bf16[1024,1152]{1,0:T(8,128)(2,1)S(1)} %bitcast.72, bf16[2304,1152]{1,0:T(8,128)(2,1)S(1)} %bitcast.75), kind=kOutput, calls=%fused_computation.34 | convolution fusion | flops 1811939328 | bytes 7274496 | tf_op jit(solution)/shard_map/dot_general | solution.py:308
  179.0 3.9 %fusion.18 = f32[1024,768]{1,0:T(8,128)} fusion(bf16[1024,1152]{1,0:T(8,128)(2,1)S(1)} %bitcast.73, bf16[2304,1152]{1,0:T(8,128)(2,1)S(1)} %bitcast.75), kind=kOutput, calls=%fused_computation.38 | convolution fusion | flops 1811939328 | bytes 7274496 | tf_op jit(solution)/shard_map/dot_general | solution.py:308
  182.9 1.8 fusion.36
  184.8 9.3 %convolution_bitcast_fusion.1 = f32[2304,1152]{1,0:T(8,128)} fusion(bf16[8,128,2304]{2,1,0:T(8,128)(2,1)S(1)} %bitcast.64, f32[8]{0:T(128)S(1)} %rsqrt_multiply_fusion, bf16[8,128,2304]{2,1,0:T(8,128)(2,1)S(1)} %get-tuple-element.23), kind=kOutput, calls=%fused_computation.2 | convolution fusion | flops 5439356928 | bytes 17695232 | tf_op jit(solution)/shard_map/dot_general | solution.py:296
  194.1 6.2 %fusion.6 = bf16[768,1152]{1,0:T(8,128)(2,1)} fusion(f32[768,1152]{1,0:T(8,128)} %convolution_bitcast_fusion.3, bf16[8,128,2304]{2,1,0:T(8,128)(2,1)} %get-tuple-element.16, bf16[8,128,2304]{2,1,0:T(8,128)(2,1)S(1)} %get-tuple-element.21, f32[8]{0:T(128)S(1)} %collective-permute-done.3), kind=kOutput, calls=%fused_computation.23 | convolution fusion | flops 1817247744 | bytes 9241088 | tf_op jit(solution)/shard_map/dot_general | solution.py:296
  200.3 0.5 collective-permute-start.7
  200.8 2.3 add_convert_fusion.1
  203.1 1.6 collective-permute-start.10
  204.7 3.4 %add_convert_fusion.2 = bf16[1024,768]{1,0:T(8,128)(2,1)} fusion(f32[1024,768]{1,0:T(8,128)S(1)} %copy-done.2, bf16[1024,1152]{1,0:T(8,128)(2,1)S(1)} %bitcast.69, bf16[2304,1152]{1,0:T(8,128)(2,1)S(1)} %bitcast.62), kind=kOutput, calls=%fused_computation.25 | convolution fusion | flops 1813512192 | bytes 8847360 | tf_op jit(solution)/shard_map/dot_general | solution.py:308
  208.1 3.4 %add_convert_fusion.3 = bf16[1024,768]{1,0:T(8,128)(2,1)} fusion(f32[1024,768]{1,0:T(8,128)S(1)} %copy-done.1, bf16[1024,1152]{1,0:T(8,128)(2,1)S(1)} %bitcast.70, bf16[2304,1152]{1,0:T(8,128)(2,1)S(1)} %bitcast.62), kind=kOutput, calls=%fused_computation.26 | convolution fusion | flops 1813512192 | bytes 8847360 | tf_op jit(solution)/shard_map/dot_general | solution.py:308
  211.5 0.5 collective-permute-start.8
  212.0 1.5 collective-permute-start.9
  213.5 10.4 %fusion = f32[2304,1152]{1,0:T(8,128)S(1)} fusion(f32[2304,1152]{1,0:T(8,128)} %convolution_bitcast_fusion.1, bf16[8,128,2304]{2,1,0:T(8,128)(2,1)} %get-tuple-element.16, bf16[8,128,2304]{2,1,0:T(8,128)(2,1)S(1)} %get-tuple-element.21, f32[8]{0:T(128)S(1)} %collective-permute-done.3), kind=kOutput, calls=%fused_computation.1 | convolution fusion | flops 5442011136 | bytes 28312064 | tf_op jit(solution)/shard_map/dot_general | solution.py:296
  223.9 10.0 %fusion.37 = f32[1024,2304]{1,0:T(8,128)} fusion(bf16[1024,1152]{1,0:T(8,128)(2,1)} %bitcast.67, bf16[2304,1152]{1,0:T(8,128)(2,1)S(1)} %bitcast.62), kind=kOutput, calls=%fused_computation.55 | convolution fusion | flops 5435817984 | bytes 17104896 | tf_op jit(solution)/shard_map/dot_general | solution.py:308
  233.9 4.8 %fusion.5 = bf16[768,1152]{1,0:T(8,128)(2,1)S(1)} fusion(f32[768,1152]{1,0:T(8,128)} %convolution_bitcast_fusion.5, bf16[8,128,2304]{2,1,0:T(8,128)(2,1)} %get-tuple-element.16, bf16[8,128,2304]{2,1,0:T(8,128)(2,1)S(1)} %get-tuple-element.21, f32[8]{0:T(128)S(1)} %collective-permute-done.3), kind=kOutput, calls=%fused_computation.22 | convolution fusion | flops 1817247744 | bytes 9241088 | tf_op jit(solution)/shard_map/dot_general | solution.py:296
  238.8 1.8 collective-permute-done.10
  240.6 1.5 collective-permute-start.6
  242.1 12.7 %convolution_add_fusion = f32[1024,2304]{1,0:T(8,128)} fusion(f32[1024,2304]{1,0:T(8,128)} %fusion.37, bf16[1024,1152]{1,0:T(8,128)(2,1)S(1)} %bitcast.66, bf16[2304,1152]{1,0:T(8,128)(2,1)} %get-tuple-element.18), kind=kOutput, calls=%fused_computation.5 | convolution fusion | flops 5438177280 | bytes 26542080 | tf_op jit(solution)/shard_map/dot_general | solution.py:308
  254.8 19.5 %collective-permute-done.8 = bf16[1024,768]{1,0:T(8,128)(2,1)} collective-permute-done((bf16[1024,768]{1,0:T(8,128)(2,1)}, bf16[1024,768]{1,0:T(8,128)(2,1)}, u32[]{:S(2)}, u32[]{:S(2)}) %collective-permute-start.8) | collective-permute-done | bytes 1572896 | tf_op jit(solution)/shard_map/ppermute | solution.py:241
  274.3 28.9 %collective-permute-done.9 = bf16[1024,768]{1,0:T(8,128)(2,1)} collective-permute-done((bf16[1024,768]{1,0:T(8,128)(2,1)}, bf16[1024,768]{1,0:T(8,128)(2,1)}, u32[]{:S(2)}, u32[]{:S(2)}) %collective-permute-start.9) | collective-permute-done | bytes 1572896 | tf_op jit(solution)/shard_map/ppermute | solution.py:241
  303.2 7.8 %add_convert_fusion = bf16[1024,2304]{1,0:T(8,128)(2,1)} fusion(f32[1024,2304]{1,0:T(8,128)} %convolution_add_fusion, bf16[1024,768]{1,0:T(8,128)(2,1)} %collective-permute-done.10, bf16[1024,768]{1,0:T(8,128)(2,1)} %collective-permute-done.9, bf16[1024,768]{1,0:T(8,128)(2,1)} %collective-permute-done.8), kind=kLoop, calls=%fused_computation.4 | loop fusion | flops 18874368 | bytes 18874368 | tf_op jit(solution)/shard_map/convert_element_type | solution.py:331
  311.0 0.0 collective-permute-done.7
  311.0 0.0 collective-permute-done.5
  311.0 5.9 %convert_add_fusion = f32[2304,1152]{1,0:T(8,128)} fusion(f32[2304,1152]{1,0:T(8,128)S(1)} %fusion, bf16[768,1152]{1,0:T(8,128)(2,1)} %collective-permute-done.7, bf16[768,1152]{1,0:T(8,128)(2,1)S(1)} %collective-permute-done.6, bf16[768,1152]{1,0:T(8,128)(2,1)} %collective-permute-done.5), kind=kLoop, calls=%fused_computation.3 | loop fusion | flops 18579456 | bytes 26542080 | tf_op jit(solution)/shard_map/add | solution.py:330
  (25 shorter events, 0.1 us)
Async XLA Ops:
  0.6 138.6 %collective-permute-start.4 = (s32[8]{0:T(128)}, s32[8]{0:T(128)S(1)}, u32[]{:S(2)}, u32[]{:S(2)}) collective-permute-start(s32[8]{0:T(128)} %param.7), channel_id=1, source_target_pairs={{0,8},{8,0},{16,24},{24,16},{1,9},{9,1},{17,25},{25,17},{2,10},{10... | collective-permute-start | bytes 104 | tf_op jit(solution)/shard_map/ppermute | solution.py:241
  4.4 1.3 copy-start
  136.1 17.3 %slice-start.2 = ((s8[4718592]{0:T(1024)(128)(4,1)}), s8[4194304]{0:T(1024)(128)(4,1)S(1)}, s32[]{:S(2)}) async-start(s8[4718592]{0:T(1024)(128)(4,1)} %bitcast.63), calls=%async_computation.2 | async-start | bytes 8388608
  136.4 1.2 collective-permute-start
  137.6 3.5 %collective-permute-start.1 = (f32[8]{0:T(128)S(1)}, f32[8]{0:T(128)S(1)}, u32[]{:S(2)}, u32[]{:S(2)}) collective-permute-start(f32[8]{0:T(128)S(1)} %add.42), channel_id=1, source_target_pairs={{0,2},{1,3},{2,0},{3,1},{4,6},{5,7},{6,4},{7,5},{8,10},{9,11},{10,... | collective-permute-start | bytes 104 | tf_op jit(solution)/shard_map/ppermute | solution.py:22
  141.1 4.4 %collective-permute-start.2 = (f32[8]{0:T(128)S(1)}, f32[8]{0:T(128)S(1)}, u32[]{:S(2)}, u32[]{:S(2)}) collective-permute-start(f32[8]{0:T(128)S(1)} %add.43), channel_id=1, source_target_pairs={{0,4},{1,5},{2,6},{3,7},{4,0},{5,1},{6,2},{7,3},{8,12},{9,13},{10,... | collective-permute-start | bytes 104 | tf_op jit(solution)/shard_map/ppermute | solution.py:22
  145.6 3.5 %collective-permute-start.3 = (f32[8]{0:T(128)S(1)}, f32[8]{0:T(128)S(1)}, u32[]{:S(2)}, u32[]{:S(2)}) collective-permute-start(f32[8]{0:T(128)S(1)} %rsqrt_multiply_fusion), channel_id=1, source_target_pairs={{0,8},{8,0},{16,24},{24,16},{1,9},{9,1},{17,25},{25,17},{2,10},{10... | collective-permute-start | bytes 104 | tf_op jit(solution)/shard_map/ppermute | solution.py:241
  149.1 4.3 %slice-start.3 = ((s8[4718592]{0:T(1024)(128)(4,1)}), s8[524288]{0:T(1024)(128)(4,1)S(1)}, s32[]{:S(2)}) async-start(s8[4718592]{0:T(1024)(128)(4,1)} %bitcast.63), calls=%async_computation.3 | async-start | bytes 1048576
  160.0 11.2 %slice-start.4 = ((s8[5308416]{0:T(1024)(128)(4,1)}), s8[4194304]{0:T(1024)(128)(4,1)S(1)}, s32[]{:S(2)}) async-start(s8[5308416]{0:T(1024)(128)(4,1)} %bitcast.74), calls=%async_computation.4 | async-start | bytes 8388608
  165.1 6.0 %slice-start.5 = ((s8[5308416]{0:T(1024)(128)(4,1)}), s8[1114112]{0:T(1024)(128)(4,1)S(1)}, s32[]{:S(2)}) async-start(s8[5308416]{0:T(1024)(128)(4,1)} %bitcast.74), calls=%async_computation.5 | async-start | bytes 2228224
  165.1 145.9 %collective-permute-start.5 = (bf16[768,1152]{1,0:T(8,128)(2,1)}, bf16[768,1152]{1,0:T(8,128)(2,1)}, u32[]{:S(2)}, u32[]{:S(2)}) collective-permute-start(bf16[768,1152]{1,0:T(8,128)(2,1)} %fusion.4), channel_id=1, source_target_pairs={{0,16},{8,24},{16,0},{24,8},{1,17},{9,25},{17,1},{25,9},{2,18},{10... | collective-permute-start | bytes 5308424 | tf_op jit(solution)/shard_map/ppermute | solution.py:245
  182.9 17.9 %slice-start = ((s8[5308416]{0:T(1024)(128)(4,1)}), s8[4194304]{0:T(1024)(128)(4,1)S(1)}, s32[]{:S(2)}) async-start(s8[5308416]{0:T(1024)(128)(4,1)} %bitcast.61), calls=%async_computation | async-start | bytes 8388608
  184.8 16.0 %slice-start.1 = ((s8[5308416]{0:T(1024)(128)(4,1)}), s8[1114112]{0:T(1024)(128)(4,1)S(1)}, s32[]{:S(2)}) async-start(s8[5308416]{0:T(1024)(128)(4,1)} %bitcast.61), calls=%async_computation.1 | async-start | bytes 2228224
  194.1 6.7 %copy-start.3 = (f32[1024,768]{1,0:T(8,128)S(1)}, f32[1024,768]{1,0:T(8,128)}, u32[]{:S(2)}) copy-start(f32[1024,768]{1,0:T(8,128)} %fusion.10) | copy-start | bytes 9437188
  200.3 110.7 %collective-permute-start.7 = (bf16[768,1152]{1,0:T(8,128)(2,1)}, bf16[768,1152]{1,0:T(8,128)(2,1)}, u32[]{:S(2)}, u32[]{:S(2)}) collective-permute-start(bf16[768,1152]{1,0:T(8,128)(2,1)} %fusion.6), channel_id=1, source_target_pairs={{0,16},{8,24},{16,0},{24,8},{1,17},{9,25},{17,1},{25,9},{2,18},{10... | collective-permute-start | bytes 5308424 | tf_op jit(solution)/shard_map/ppermute | solution.py:245
  200.8 3.8 %copy-start.2 = (f32[1024,768]{1,0:T(8,128)S(1)}, f32[1024,768]{1,0:T(8,128)}, u32[]{:S(2)}) copy-start(f32[1024,768]{1,0:T(8,128)} %fusion.14) | copy-start | bytes 9437188
  203.1 5.0 %copy-start.1 = (f32[1024,768]{1,0:T(8,128)S(1)}, f32[1024,768]{1,0:T(8,128)}, u32[]{:S(2)}) copy-start(f32[1024,768]{1,0:T(8,128)} %fusion.18) | copy-start | bytes 9437188
  203.1 37.5 %collective-permute-start.10 = (bf16[1024,768]{1,0:T(8,128)(2,1)S(1)}, bf16[1024,768]{1,0:T(8,128)(2,1)}, u32[]{:S(2)}, u32[]{:S(2)}) collective-permute-start(bf16[1024,768]{1,0:T(8,128)(2,1)S(1)} %add_convert_fusion.1), channel_id=1, source_target_pairs={{0,8},{8,0},{16,24},{24,16},{1,9},{9,1},{17,25},{25,17},{2,10},{10... | collective-permute-start | bytes 4718600 | tf_op jit(solution)/shard_map/ppermute | solution.py:241
  211.5 62.8 %collective-permute-start.8 = (bf16[1024,768]{1,0:T(8,128)(2,1)}, bf16[1024,768]{1,0:T(8,128)(2,1)}, u32[]{:S(2)}, u32[]{:S(2)}) collective-permute-start(bf16[1024,768]{1,0:T(8,128)(2,1)} %add_convert_fusion.3), channel_id=1, source_target_pairs={{0,8},{8,0},{16,24},{24,16},{1,9},{9,1},{17,25},{25,17},{2,10},{10... | collective-permute-start | bytes 4718600 | tf_op jit(solution)/shard_map/ppermute | solution.py:241
  212.0 91.1 %collective-permute-start.9 = (bf16[1024,768]{1,0:T(8,128)(2,1)}, bf16[1024,768]{1,0:T(8,128)(2,1)}, u32[]{:S(2)}, u32[]{:S(2)}) collective-permute-start(bf16[1024,768]{1,0:T(8,128)(2,1)} %add_convert_fusion.2), channel_id=1, source_target_pairs={{0,8},{8,0},{16,24},{24,16},{1,9},{9,1},{17,25},{25,17},{2,10},{10... | collective-permute-start | bytes 4718600 | tf_op jit(solution)/shard_map/ppermute | solution.py:241
  240.6 70.4 %collective-permute-start.6 = (bf16[768,1152]{1,0:T(8,128)(2,1)S(1)}, bf16[768,1152]{1,0:T(8,128)(2,1)S(1)}, u32[]{:S(2)}, u32[]{:S(2)}) collective-permute-start(bf16[768,1152]{1,0:T(8,128)(2,1)S(1)} %fusion.5), channel_id=1, source_target_pairs={{0,16},{8,24},{16,0},{24,8},{1,17},{9,25},{17,1},{25,9},{2,18},{10... | collective-permute-start | bytes 5308424 | tf_op jit(solution)/shard_map/ppermute | solution.py:245

commit v4 on v3

--- a/solution.py
+++ b/solution.py
@@ -288,7 +288,7 @@
     masked = [masked_by(whole[k], keeps[k]) for k in range(inner)]
     tokens = seqs * seq_len
 
-    def grad_w(m, lo, hi):
+    def grad_w(m, lo, hi, hid_parts):
         total = None
         for k in range(inner):
             part = masked[k][:, :, m * share:(m + 1) * share]
@@ -315,14 +315,20 @@
         return total
 
     cuts = pieces(units, 3)
-    w_terms = [[grad_w(m, *cut).astype(BF16) for m in range(1, outer)] for cut in cuts]
+    w_first = [grad_w(m, *cuts[0], hid_parts).astype(BF16) for m in range(1, outer)]
+    others, w_first = lax.optimization_barrier((masked[1:], w_first))
+    h_terms = []
+    for cut in cuts:
+        terms = [grad_h(value, *cut).astype(BF16) for value in others]
+        others, terms = lax.optimization_barrier((others, terms))
+        h_terms.append(terms)
+    w_terms = [w_first] + [
+        [grad_w(m, *cut, hid_parts).astype(BF16) for m in range(1, outer)] for cut in cuts[1:]
+    ]
     grad_w_in = [[along_outer(terms[m - 1], -m) for m in range(1, outer)] for terms in w_terms]
-    others, w_terms[0] = lax.optimization_barrier((masked[1:], w_terms[0]))
-    grad_h_in = [
-        [along_inner(grad_h(others[k - 1], *cut).astype(BF16), -k) for k in range(1, inner)] for cut in cuts
-    ]
-
-    own_w, own_h = lax.optimization_barrier((grad_w(0, 0, units), grad_h(masked[0], 0, units)))
+    grad_h_in = [[along_inner(terms[k - 1], -k) for k in range(1, inner)] for terms in h_terms]
+
+    own_w, own_h = lax.optimization_barrier((grad_w(0, 0, units, hid_parts), grad_h(masked[0], 0, units)))
     own_w = with_layout_constraint(own_w, Layout(major_to_minor=(0, 1)))
     for k in range(inner - 1):
         own_h = own_h + jnp.concatenate([parts[k] for parts in grad_h_in], axis=1).astype(F32)

time: 317 us -> 315 us (level)
  waiting for transfers between devices: 57 us -> 50.8 us
    ppermute x5, waiting for transfers between devices: 52.2 us -> 46 us  [along_inner(): return lax.ppermute(value, 'dp', perm)]
    dot_general x8, matrix products: 46.5 us -> 51.7 us  [grad_w(): lax.dot_general(hid_parts[k][:, :, lo:hi].reshape(tokens, hi - lo), scale...]
    dot_general x8, matrix products: 43.6 us -> 38.8 us  [grad_h(): lax.dot_general(source[:, :, m * share:(m + 1) * share].reshape(tokens, s...]
  transfers between devices with their start and end apart: 11 -> 11, of which waited for: 7 -> 6; matrix products, arithmetic and copies ran while one was open for 28% -> 22% of each run, Pallas kernels for 41% -> 42%
where the time goes in v4:
time: 315 us; the launch traced here: 313 us
  Pallas kernels  130 us (41%)
  matrix products  90.5 us (29%)
  waiting for transfers between devices  50.8 us (16%)
  other arithmetic  19.1 us (6%)
  starting transfers between devices  16.1 us (5%)
  local copies, waits for them, and re-layouts  5.03 us (2%)
    pallas_call x1, Pallas kernels, exchange(): pl.pallas_call(functools.partial(exchange_kernel, ranks), out_shape=(jax....  130 us
    dot_general x8, matrix products, grad_w(): lax.dot_general(hid_parts[k][:, :, lo:hi].reshape(tokens, hi - lo), scale...  51.7 us
    ppermute x5, waiting for transfers between devices, along_inner(): return lax.ppermute(value, 'dp', perm)  46 us
    dot_general x8, matrix products, grad_h(): lax.dot_general(source[:, :, m * share:(m + 1) * share].reshape(tokens, s...  38.8 us
    ppermute x5, starting transfers between devices, along_inner(): return lax.ppermute(value, 'dp', perm)  8.28 us
    convert_element_type x1, other arithmetic, body(): return (own_w, own_h.astype(BF16).reshape(seqs, seq_len, units))  7.84 us
  transfers between devices with their start and end apart: 11, of which 6 were waited for; matrix products, arithmetic and copies ran while one was open for 22% of the time, Pallas kernels for 42%

profile of v4, /device:TPU:0, one launch (start us, length us, event | category | flops | bytes accessed | tf_op | source)
XLA Modules:
  0.0 312.8 jit_solution(11118966396483666033)
XLA Ops:
  0.6 3.0 collective-permute-start.4
  3.6 0.8 iota_compare_fusion.1
  4.4 1.3 copy-done
  5.7 130.4 %shard_map.59 = (bf16[16,128,2304]{2,1,0:T(8,128)(2,1)}, bf16[8,128,2304]{2,1,0:T(8,128)(2,1)}, bf16[2304,1152]{1,0:T(8,128)(2,1)}, f32[8,128,128]{2,1,0:T(8,128)S(1)}) custom-call(bf16[8,16,4608]{2,1,0:T(8,128)(2,1)S(1)} %copy-done, bf16[8,128,2304]{2,1,0:T(8,128)(2,1)} %hid.1, bf16[2304,1152]{1,0:T(8,128)(2,1)} %w.1), custom_call_target="tpu_custom_call" | custom-call | tf_op jit(solution)/shard_map/pallas_call | solution.py:202
  136.1 0.0 slice-start.2
  136.1 0.3 select_reduce_fusion
  136.4 0.1 collective-permute-start
  136.4 1.1 collective-permute-done
  137.5 1.6 collective-permute-start.1
  139.2 0.0 collective-permute-done.4
  139.2 0.1 iota_compare_fusion
  139.2 1.9 collective-permute-done.1
  141.1 2.6 collective-permute-start.2
  143.7 1.8 collective-permute-done.2
  145.5 1.6 collective-permute-start.3
  147.1 1.9 collective-permute-done.3
  149.1 4.2 %bitcast_select_fusion = (bf16[8,128,2304]{2,1,0:T(8,128)(2,1)S(1)}, bf16[8,128,2304]{2,1,0:T(8,128)(2,1)S(1)}) fusion(bf16[2,8,128,2304]{3,2,1,0:T(8,128)(2,1)} %bitcast.64, pred[8,128]{1,0:T(8,128)(4,1)S(1)} %iota_compare_fusion, pred[8,128]{1,0:T(8,128)(4,1)S(1)} %iota_compare_fusion.1), kind=kLoop, calls=%fused_computation.6 | loop fusion | flops 4718592 | bytes 18876416 | tf_op jit(solution)/shard_map/jit(_where)/select_n | solution.py:252
  153.3 2.5 convolution_bitcast_fusion.3
  155.8 2.5 convolution_bitcast_fusion.7
  158.3 4.2 %convolution_bitcast_fusion.5 = f32[768,1152]{1,0:T(8,128)} fusion(bf16[8,128,2304]{2,1,0:T(8,128)(2,1)S(1)} %bitcast.68, f32[8]{0:T(128)S(1)} %rsqrt_multiply_fusion, bf16[8,128,2304]{2,1,0:T(8,128)(2,1)S(1)} %get-tuple-element.35), kind=kOutput, calls=%fused_computation.17 | convolution fusion | flops 1815478272 | bytes 7471616 | tf_op jit(solution)/shard_map/dot_general | solution.py:296
  162.5 1.8 fusion.38
  164.3 19.9 %convolution_bitcast_fusion.1 = f32[2304,1152]{1,0:T(8,128)} fusion(bf16[8,128,2304]{2,1,0:T(8,128)(2,1)S(1)} %bitcast.68, f32[8]{0:T(128)S(1)} %rsqrt_multiply_fusion, bf16[8,128,2304]{2,1,0:T(8,128)(2,1)S(1)} %get-tuple-element.35), kind=kOutput, calls=%fused_computation.2 | convolution fusion | flops 5439356928 | bytes 17695232 | tf_op jit(solution)/shard_map/dot_general | solution.py:296
  184.2 3.7 %fusion.6 = bf16[768,1152]{1,0:T(8,128)(2,1)} fusion(f32[768,1152]{1,0:T(8,128)S(1)} %convolution_bitcast_fusion.3, bf16[8,128,2304]{2,1,0:T(8,128)(2,1)S(1)} %bitcast.81, bf16[8,128,2304]{2,1,0:T(8,128)(2,1)S(1)} %get-tuple-element.32, f32[8]{0:T(128)S(1)} %collective-permute-done.3), kind=kOutput, calls=%fused_computation.23 | convolution fusion | flops 1817247744 | bytes 9241088 | tf_op jit(solution)/shard_map/dot_general | solution.py:296
  187.9 1.5 collective-permute-start.7
  189.4 3.8 %fusion.4 = bf16[768,1152]{1,0:T(8,128)(2,1)} fusion(f32[768,1152]{1,0:T(8,128)S(1)} %convolution_bitcast_fusion.7, bf16[8,128,2304]{2,1,0:T(8,128)(2,1)S(1)} %bitcast.81, bf16[8,128,2304]{2,1,0:T(8,128)(2,1)S(1)} %get-tuple-element.32, f32[8]{0:T(128)S(1)} %collective-permute-done.3), kind=kOutput, calls=%fused_computation.21 | convolution fusion | flops 1817247744 | bytes 9241088 | tf_op jit(solution)/shard_map/dot_general | solution.py:296
  193.2 0.5 collective-permute-start.5
  193.7 0.6 fusion.37
  194.4 0.0 slice-start.1
  194.4 2.2 fusion.18
  196.7 2.3 add_convert_fusion.3
  198.9 1.7 collective-permute-start.8
  200.6 0.6 fusion.36
  201.2 2.2 fusion.14
  203.5 3.5 %add_convert_fusion.2 = bf16[1024,768]{1,0:T(8,128)(2,1)} fusion(f32[1024,768]{1,0:T(8,128)S(1)} %fusion.14, bf16[1024,1152]{1,0:T(8,128)(2,1)S(1)} %bitcast.74, bf16[2304,1152]{1,0:T(8,128)(2,1)S(1)} %bitcast.66), kind=kOutput, calls=%fused_computation.25 | convolution fusion | flops 1813512192 | bytes 8847360 | tf_op jit(solution)/shard_map/dot_general | solution.py:308
  207.0 0.4 collective-permute-start.9
  207.4 0.6 fusion.35
  208.1 2.2 fusion.10
  210.3 3.6 %add_convert_fusion.1 = bf16[1024,768]{1,0:T(8,128)(2,1)} fusion(f32[1024,768]{1,0:T(8,128)S(1)} %fusion.10, bf16[1024,1152]{1,0:T(8,128)(2,1)S(1)} %bitcast.75, bf16[2304,1152]{1,0:T(8,128)(2,1)S(1)} %bitcast.66), kind=kOutput, calls=%fused_computation.24 | convolution fusion | flops 1813512192 | bytes 8847360 | tf_op jit(solution)/shard_map/dot_general | solution.py:308
  213.9 1.6 collective-permute-start.10
  215.5 10.4 %fusion = f32[2304,1152]{1,0:T(8,128)S(1)} fusion(f32[2304,1152]{1,0:T(8,128)} %convolution_bitcast_fusion.1, bf16[8,128,2304]{2,1,0:T(8,128)(2,1)} %get-tuple-element.22, bf16[8,128,2304]{2,1,0:T(8,128)(2,1)S(1)} %get-tuple-element.32, f32[8]{0:T(128)S(1)} %collective-permute-done.3), kind=kOutput, calls=%fused_computation.1 | convolution fusion | flops 5442011136 | bytes 28312064 | tf_op jit(solution)/shard_map/dot_general | solution.py:296
  225.9 10.0 %fusion.39 = f32[1024,2304]{1,0:T(8,128)} fusion(bf16[1024,1152]{1,0:T(8,128)(2,1)} %bitcast.71, bf16[2304,1152]{1,0:T(8,128)(2,1)S(1)} %bitcast.66), kind=kOutput, calls=%fused_computation.57 | convolution fusion | flops 5435817984 | bytes 17104896 | tf_op jit(solution)/shard_map/dot_general | solution.py:308
  235.9 4.8 %fusion.5 = bf16[768,1152]{1,0:T(8,128)(2,1)S(1)} fusion(f32[768,1152]{1,0:T(8,128)} %convolution_bitcast_fusion.5, bf16[8,128,2304]{2,1,0:T(8,128)(2,1)} %get-tuple-element.22, bf16[8,128,2304]{2,1,0:T(8,128)(2,1)S(1)} %get-tuple-element.32, f32[8]{0:T(128)S(1)} %collective-permute-done.3), kind=kOutput, calls=%fused_computation.22 | convolution fusion | flops 1817247744 | bytes 9241088 | tf_op jit(solution)/shard_map/dot_general | solution.py:296
  240.7 1.5 collective-permute-start.6
  242.3 12.7 %convolution_add_fusion = f32[1024,2304]{1,0:T(8,128)} fusion(f32[1024,2304]{1,0:T(8,128)} %fusion.39, bf16[1024,1152]{1,0:T(8,128)(2,1)S(1)} %bitcast.70, bf16[2304,1152]{1,0:T(8,128)(2,1)} %get-tuple-element.24), kind=kOutput, calls=%fused_computation.5 | convolution fusion | flops 5438177280 | bytes 26542080 | tf_op jit(solution)/shard_map/dot_general | solution.py:308
  255.0 15.2 %collective-permute-done.9 = bf16[1024,768]{1,0:T(8,128)(2,1)} collective-permute-done((bf16[1024,768]{1,0:T(8,128)(2,1)}, bf16[1024,768]{1,0:T(8,128)(2,1)}, u32[]{:S(2)}, u32[]{:S(2)}) %collective-permute-start.9) | collective-permute-done | bytes 1572896 | tf_op jit(solution)/shard_map/ppermute | solution.py:241
  270.2 28.9 %collective-permute-done.10 = bf16[1024,768]{1,0:T(8,128)(2,1)} collective-permute-done((bf16[1024,768]{1,0:T(8,128)(2,1)}, bf16[1024,768]{1,0:T(8,128)(2,1)}, u32[]{:S(2)}, u32[]{:S(2)}) %collective-permute-start.10) | collective-permute-done | bytes 1572896 | tf_op jit(solution)/shard_map/ppermute | solution.py:241
  299.1 7.8 %add_convert_fusion = bf16[1024,2304]{1,0:T(8,128)(2,1)} fusion(f32[1024,2304]{1,0:T(8,128)} %convolution_add_fusion, bf16[1024,768]{1,0:T(8,128)(2,1)} %collective-permute-done.10, bf16[1024,768]{1,0:T(8,128)(2,1)} %collective-permute-done.9, bf16[1024,768]{1,0:T(8,128)(2,1)} %collective-permute-done.8), kind=kLoop, calls=%fused_computation.4 | loop fusion | flops 18874368 | bytes 18874368 | tf_op jit(solution)/shard_map/convert_element_type | solution.py:337
  306.9 5.9 %convert_add_fusion = f32[2304,1152]{1,0:T(8,128)} fusion(f32[2304,1152]{1,0:T(8,128)S(1)} %fusion, bf16[768,1152]{1,0:T(8,128)(2,1)} %collective-permute-done.7, bf16[768,1152]{1,0:T(8,128)(2,1)S(1)} %collective-permute-done.6, bf16[768,1152]{1,0:T(8,128)(2,1)} %collective-permute-done.5), kind=kLoop, calls=%fused_computation.3 | loop fusion | flops 18579456 | bytes 26542080 | tf_op jit(solution)/shard_map/add | solution.py:336
  (26 shorter events, 0.1 us)
Async XLA Ops:
  0.6 138.5 %collective-permute-start.4 = (s32[8]{0:T(128)}, s32[8]{0:T(128)S(1)}, u32[]{:S(2)}, u32[]{:S(2)}) collective-permute-start(s32[8]{0:T(128)} %param.7), channel_id=1, source_target_pairs={{0,8},{8,0},{16,24},{24,16},{1,9},{9,1},{17,25},{25,17},{2,10},{10... | collective-permute-start | bytes 104 | tf_op jit(solution)/shard_map/ppermute | solution.py:241
  4.4 1.3 copy-start
  136.1 17.3 %slice-start.2 = ((s8[4718592]{0:T(1024)(128)(4,1)}), s8[4194304]{0:T(1024)(128)(4,1)S(1)}, s32[]{:S(2)}) async-start(s8[4718592]{0:T(1024)(128)(4,1)} %bitcast.67), calls=%async_computation.2 | async-start | bytes 8388608
  136.4 1.2 collective-permute-start
  137.5 3.5 %collective-permute-start.1 = (f32[8]{0:T(128)S(1)}, f32[8]{0:T(128)S(1)}, u32[]{:S(2)}, u32[]{:S(2)}) collective-permute-start(f32[8]{0:T(128)S(1)} %add.42), channel_id=1, source_target_pairs={{0,2},{1,3},{2,0},{3,1},{4,6},{5,7},{6,4},{7,5},{8,10},{9,11},{10,... | collective-permute-start | bytes 104 | tf_op jit(solution)/shard_map/ppermute | solution.py:22
  141.1 4.4 %collective-permute-start.2 = (f32[8]{0:T(128)S(1)}, f32[8]{0:T(128)S(1)}, u32[]{:S(2)}, u32[]{:S(2)}) collective-permute-start(f32[8]{0:T(128)S(1)} %add.43), channel_id=1, source_target_pairs={{0,4},{1,5},{2,6},{3,7},{4,0},{5,1},{6,2},{7,3},{8,12},{9,13},{10,... | collective-permute-start | bytes 104 | tf_op jit(solution)/shard_map/ppermute | solution.py:22
  145.5 3.5 %collective-permute-start.3 = (f32[8]{0:T(128)S(1)}, f32[8]{0:T(128)S(1)}, u32[]{:S(2)}, u32[]{:S(2)}) collective-permute-start(f32[8]{0:T(128)S(1)} %rsqrt_multiply_fusion), channel_id=1, source_target_pairs={{0,8},{8,0},{16,24},{24,16},{1,9},{9,1},{17,25},{25,17},{2,10},{10... | collective-permute-start | bytes 104 | tf_op jit(solution)/shard_map/ppermute | solution.py:241
  149.1 4.3 %slice-start.3 = ((s8[4718592]{0:T(1024)(128)(4,1)}), s8[524288]{0:T(1024)(128)(4,1)S(1)}, s32[]{:S(2)}) async-start(s8[4718592]{0:T(1024)(128)(4,1)} %bitcast.67), calls=%async_computation.3 | async-start | bytes 1048576
  162.5 21.7 %slice-start.6 = ((s8[4718592]{0:T(1024)(128)(4,1)}), s8[4194304]{0:T(1024)(128)(4,1)S(1)}, s32[]{:S(2)}) async-start(s8[4718592]{0:T(1024)(128)(4,1)} %bitcast.80), calls=%async_computation.6 | async-start | bytes 8388608
  164.3 19.9 %slice-start.7 = ((s8[4718592]{0:T(1024)(128)(4,1)}), s8[524288]{0:T(1024)(128)(4,1)S(1)}, s32[]{:S(2)}) async-start(s8[4718592]{0:T(1024)(128)(4,1)} %bitcast.80), calls=%async_computation.7 | async-start | bytes 1048576
  184.2 10.2 %slice-start.4 = ((s8[5308416]{0:T(1024)(128)(4,1)}), s8[4194304]{0:T(1024)(128)(4,1)S(1)}, s32[]{:S(2)}) async-start(s8[5308416]{0:T(1024)(128)(4,1)} %bitcast.78), calls=%async_computation.4 | async-start | bytes 8388608
  187.9 6.5 %slice-start.5 = ((s8[5308416]{0:T(1024)(128)(4,1)}), s8[1114112]{0:T(1024)(128)(4,1)S(1)}, s32[]{:S(2)}) async-start(s8[5308416]{0:T(1024)(128)(4,1)} %bitcast.78), calls=%async_computation.5 | async-start | bytes 2228224
  187.9 119.0 %collective-permute-start.7 = (bf16[768,1152]{1,0:T(8,128)(2,1)}, bf16[768,1152]{1,0:T(8,128)(2,1)}, u32[]{:S(2)}, u32[]{:S(2)}) collective-permute-start(bf16[768,1152]{1,0:T(8,128)(2,1)} %fusion.6), channel_id=1, source_target_pairs={{0,16},{8,24},{16,0},{24,8},{1,17},{9,25},{17,1},{25,9},{2,18},{10... | collective-permute-start | bytes 5308424 | tf_op jit(solution)/shard_map/ppermute | solution.py:245
  193.2 113.7 %collective-permute-start.5 = (bf16[768,1152]{1,0:T(8,128)(2,1)}, bf16[768,1152]{1,0:T(8,128)(2,1)}, u32[]{:S(2)}, u32[]{:S(2)}) collective-permute-start(bf16[768,1152]{1,0:T(8,128)(2,1)} %fusion.4), channel_id=1, source_target_pairs={{0,16},{8,24},{16,0},{24,8},{1,17},{9,25},{17,1},{25,9},{2,18},{10... | collective-permute-start | bytes 5308424 | tf_op jit(solution)/shard_map/ppermute | solution.py:245
  193.7 2.9 slice-start
  194.4 2.3 slice-start.1
  198.9 41.8 %collective-permute-start.8 = (bf16[1024,768]{1,0:T(8,128)(2,1)S(1)}, bf16[1024,768]{1,0:T(8,128)(2,1)}, u32[]{:S(2)}, u32[]{:S(2)}) collective-permute-start(bf16[1024,768]{1,0:T(8,128)(2,1)S(1)} %add_convert_fusion.3), channel_id=1, source_target_pairs={{0,8},{8,0},{16,24},{24,16},{1,9},{9,1},{17,25},{25,17},{2,10},{10... | collective-permute-start | bytes 4718600 | tf_op jit(solution)/shard_map/ppermute | solution.py:241
  207.0 63.2 %collective-permute-start.9 = (bf16[1024,768]{1,0:T(8,128)(2,1)}, bf16[1024,768]{1,0:T(8,128)(2,1)}, u32[]{:S(2)}, u32[]{:S(2)}) collective-permute-start(bf16[1024,768]{1,0:T(8,128)(2,1)} %add_convert_fusion.2), channel_id=1, source_target_pairs={{0,8},{8,0},{16,24},{24,16},{1,9},{9,1},{17,25},{25,17},{2,10},{10... | collective-permute-start | bytes 4718600 | tf_op jit(solution)/shard_map/ppermute | solution.py:241
  213.9 85.2 %collective-permute-start.10 = (bf16[1024,768]{1,0:T(8,128)(2,1)}, bf16[1024,768]{1,0:T(8,128)(2,1)}, u32[]{:S(2)}, u32[]{:S(2)}) collective-permute-start(bf16[1024,768]{1,0:T(8,128)(2,1)} %add_convert_fusion.1), channel_id=1, source_target_pairs={{0,8},{8,0},{16,24},{24,16},{1,9},{9,1},{17,25},{25,17},{2,10},{10... | collective-permute-start | bytes 4718600 | tf_op jit(solution)/shard_map/ppermute | solution.py:241
  240.7 66.2 %collective-permute-start.6 = (bf16[768,1152]{1,0:T(8,128)(2,1)S(1)}, bf16[768,1152]{1,0:T(8,128)(2,1)S(1)}, u32[]{:S(2)}, u32[]{:S(2)}) collective-permute-start(bf16[768,1152]{1,0:T(8,128)(2,1)S(1)} %fusion.5), channel_id=1, source_target_pairs={{0,16},{8,24},{16,0},{24,8},{1,17},{9,25},{17,1},{25,9},{2,18},{10... | collective-permute-start | bytes 5308424 | tf_op jit(solution)/shard_map/ppermute | solution.py:245
